TPU v7x, 32 devices: a whole 2x2x4 slice. The times are simulated.
32 devices in a mesh: groups: 2 (over y), expert: 8 (over z, x), tensor: 2 (over core).
Axes of the slice: x: 2, y: 2, z: 4, core: 2. Of those that a mesh axis runs over, the one named last changes fastest.
Arguments:
- conv_input: bfloat16 [32, 8192], P(('groups', 'expert'), 'tensor'), parts along dimension 0, may hold values from -6 to 6
- gate_input: bfloat16 [32, 8192], P(('groups', 'expert'), 'tensor'), parts along dimension 0, may hold values from -6 to 6
- step_input: bfloat16 [32, 8192], P(('groups', 'expert'), 'tensor'), parts along dimension 0, may hold values from -6 to 6
- b_proj: float32 [32, 16], P(('groups', 'expert')), parts along dimension 0, may hold values from -6 to 6
- c_proj: float32 [32, 16], P(('groups', 'expert')), parts along dimension 0, may hold values from -6 to 6
- slot_ids: int32 [32], P(('groups', 'expert')), parts along dimension 0, may hold values from 0 to 15, as said below
- state_pool: bfloat16 [32, 16, 8192], P(('groups', 'expert'), None, 'tensor'), parts along dimension 0, may hold values from -6 to 6
- conv_pool: bfloat16 [32, 3, 8192], P(('groups', 'expert'), None, 'tensor'), parts along dimension 0, may hold values from -6 to 6
- conv_weight: float32 [4, 8192], P(None, 'tensor'), may hold values from -4 to 4
- conv_bias: float32 [8192], P('tensor'), may hold values from -4 to 4
- step_bias: float32 [8192], P('tensor'), may hold values from -4 to 0
- a_log: float32 [16, 8192], P(None, 'tensor'), may hold values from -1 to 2.5
- d_skip: float32 [8192], P('tensor'), may hold values from 0.5 to 1.5
- out_weight: bfloat16 [8192, 4096], P('tensor', 'expert'), may hold values from -0.0625 to 0.0625
- residual: bfloat16 [32, 4096], P(('groups', 'expert')), parts along dimension 0, may hold values from -6 to 6
- norm_gain: float32 [4096], replicated, may hold values from 0.5 to 1.5
- expert_ids: int32 [32, 2], P(('groups', 'expert')), parts along dimension 0, may hold values from 0 to 2, all different within a row
- expert_probs: bfloat16 [32, 2], P(('groups', 'expert')), parts along dimension 0, may hold values from 0.19921875 to 1
- gate_weight: bfloat16 [36864, 4096], P(('expert', 'tensor')), may hold values from -0.09375 to 0.09375
- up_weight: bfloat16 [36864, 4096], P(('expert', 'tensor')), may hold values from -0.09375 to 0.09375
- down_weight: bfloat16 [36864, 4096], P(('expert', 'tensor')), may hold values from -0.0546875 to 0.0546875
Outputs:
- layer_out: bfloat16 [32, 4096], P(('groups', 'expert')), parts along dimension 0
- new_state: bfloat16 [32, 16, 8192], P(('groups', 'expert'), None, 'tensor'), parts along dimension 0
There are 2 independent parts, one for each index of `groups`. A program takes and returns all parts, laid end to end along the dimension named above; an argument that names none is the same for every part. Nothing has to cross between parts.
Inputs may be any that keep to these rules, and one draw needn't show every extreme that they name: `slot_ids`: the rows of one index of expert (rows d*2 to (d+1)*2 - 1) use distinct slots among d*2 to (d+1)*2 - 1. `expert_ids`: each row names two different experts.
All inputs are finite; a program needn't handle non-finite values.
Results may differ from a plain program's by a relative error of at most 0.0063.
Values may be sent and summed in bfloat16 or wider, within the bound.
No kernel may reach another device: no remote copies, remote signals or barrier semaphores. Data moves between devices by JAX's collectives and lax.ppermute only.
A program may use at most 128 MiB of HBM per device.

v0:
```python
import jax
import jax.numpy as jnp
from jax import lax
from jax.sharding import PartitionSpec as P

EXPERTS = 3
FF = 12288


def mamba_step(
    states,
    history,
    conv_input,
    gate_input,
    step_input,
    b_proj,
    c_proj,
    conv_weight,
    conv_bias,
    step_bias,
    a_log,
    d_skip,
):
    inputs = conv_input.astype(jnp.float32)
    conv_sum = conv_weight[-1] * inputs + conv_bias
    for lag in range(history.shape[1]):
        conv_sum = conv_sum + conv_weight[lag] * history[:, lag]
    conv_out = jax.nn.silu(conv_sum)
    step_size = jax.nn.softplus(step_input.astype(jnp.float32) + step_bias)
    state_rates = -jnp.exp(a_log)
    decay_rate = jnp.exp(step_size[:, None, :] * state_rates[None])
    state_next = decay_rate * states + (step_size * conv_out)[:, None, :] * b_proj[:, :, None]
    output = jnp.sum(c_proj[:, :, None] * state_next, axis=1) + d_skip * conv_out
    gated_out = (output * jax.nn.silu(gate_input.astype(jnp.float32))).astype(jnp.bfloat16)
    return (state_next, gated_out)


def expert_terms(rows, coefs, first_unit, gate_weight, up_weight, down_weight):
    dims = (((1,), (1,)), ((), ()))
    gate_act = lax.dot_general(rows, gate_weight, dims, preferred_element_type=jnp.float32)
    up_act = lax.dot_general(rows, up_weight, dims, preferred_element_type=jnp.float32)
    hidden = (jax.nn.silu(gate_act) * up_act).astype(jnp.bfloat16)
    units = gate_weight.shape[0]
    lower_expert = first_unit // FF
    boundary = (lower_expert + 1) * FF - first_unit
    column = jnp.arange(units, dtype=jnp.int32)[None, :]
    zeros_bf = jnp.zeros_like(hidden)
    lower_hidden = jnp.where(column < boundary, hidden, zeros_bf)
    upper_hidden = jnp.where(column >= boundary, hidden, zeros_bf)
    expert_range = jnp.arange(EXPERTS, dtype=jnp.int32)[None, :]
    wide_coefs = coefs.astype(jnp.float32)
    lower_coef = jnp.sum(wide_coefs * (expert_range == lower_expert).astype(jnp.float32), axis=1)
    upper_coef = jnp.sum(
        wide_coefs * (expert_range == lower_expert + 1).astype(jnp.float32), axis=1
    )
    lower_out = jnp.dot(lower_hidden, down_weight, preferred_element_type=jnp.float32)
    upper_out = jnp.dot(upper_hidden, down_weight, preferred_element_type=jnp.float32)
    return lower_coef[:, None] * lower_out + upper_coef[:, None] * upper_out


def local(
    conv_input,
    gate_input,
    step_input,
    b_proj,
    c_proj,
    slot_ids,
    state_pool,
    conv_pool,
    conv_weight,
    conv_bias,
    step_bias,
    a_log,
    d_skip,
    out_weight,
    residual,
    norm_gain,
    expert_ids,
    expert_probs,
    gate_weight,
    up_weight,
    down_weight,
):
    pool_dev = state_pool.shape[0]
    local_slot = slot_ids - lax.axis_index("expert") * pool_dev
    select = (local_slot[:, None] == jnp.arange(pool_dev, dtype=jnp.int32)[None, :]).astype(
        jnp.bfloat16
    )
    states = jnp.einsum("rp,pnc->rnc", select, state_pool, preferred_element_type=jnp.float32)
    history = jnp.einsum("rp,pkc->rkc", select, conv_pool, preferred_element_type=jnp.float32)
    state_next, gated_out = mamba_step(
        states,
        history,
        conv_input,
        gate_input,
        step_input,
        b_proj,
        c_proj,
        conv_weight,
        conv_bias,
        step_bias,
        a_log,
        d_skip,
    )
    columns = jnp.dot(
        lax.all_gather(gated_out, "expert", axis=0, tiled=True),
        out_weight,
        preferred_element_type=jnp.float32,
    )
    returned_cols = lax.all_to_all(columns, "expert", split_axis=0, concat_axis=1, tiled=True)
    mixed = lax.psum(returned_cols, "tensor").astype(jnp.bfloat16)
    hidden_state = (residual.astype(jnp.float32) + mixed.astype(jnp.float32)).astype(jnp.bfloat16)
    wide = hidden_state.astype(jnp.float32)
    normed = (
        wide * lax.rsqrt(jnp.mean(wide * wide, axis=1, keepdims=True) + 1e-05) * norm_gain
    ).astype(jnp.bfloat16)
    probs = expert_probs.astype(jnp.float32)
    expert_range = jnp.arange(EXPERTS, dtype=jnp.int32)
    picked = (expert_ids[:, :, None] == expert_range[None, None, :]).astype(jnp.float32)
    coefs = jnp.sum(picked * probs[:, :, None], axis=1).astype(jnp.bfloat16)
    units = gate_weight.shape[0]
    first_unit = (
        lax.axis_index("expert") * lax.axis_size("tensor") + lax.axis_index("tensor")
    ) * units
    peers = lax.axis_size("expert")
    span = EXPERTS * FF // peers
    dest = jnp.arange(peers, dtype=jnp.int32)[:, None]
    intersection = (
        (expert_range[None, :] * FF < (dest + 1) * span)
        & ((expert_range[None, :] + 1) * FF > dest * span)
    ).astype(jnp.float32)
    chosen = jnp.sum(picked, axis=1)
    needed = jnp.dot(intersection, chosen.T, preferred_element_type=jnp.float32) > 0.5
    outgoing = jnp.where(needed[:, :, None], normed[None], jnp.zeros_like(normed)[None])
    out_coefs = jnp.broadcast_to(coefs[None], (peers, coefs.shape[0], coefs.shape[1]))
    rows_in = lax.all_to_all(outgoing, "expert", split_axis=0, concat_axis=0, tiled=True)
    coefs_in = lax.all_to_all(out_coefs, "expert", split_axis=0, concat_axis=0, tiled=True)
    flat_rows = rows_in.reshape(-1, rows_in.shape[2])
    flat_coefs = coefs_in.reshape(-1, coefs_in.shape[2])
    result = expert_terms(flat_rows, flat_coefs, first_unit, gate_weight, up_weight, down_weight)
    partial_value = result.reshape(rows_in.shape[0], rows_in.shape[1], rows_in.shape[2])
    returned = lax.all_to_all(partial_value, "expert", split_axis=0, concat_axis=0, tiled=True)
    routed = lax.psum(jnp.sum(returned, axis=0), "tensor")
    layer_out = (hidden_state.astype(jnp.float32) + routed).astype(jnp.bfloat16)
    return (layer_out, state_next.astype(jnp.bfloat16))


def solution(mesh):
    return jax.shard_map(
        local,
        mesh=mesh,
        in_specs=(
            P(("groups", "expert"), "tensor"),
            P(("groups", "expert"), "tensor"),
            P(("groups", "expert"), "tensor"),
            P(("groups", "expert"), None),
            P(("groups", "expert"), None),
            P(("groups", "expert")),
            P(("groups", "expert"), None, "tensor"),
            P(("groups", "expert"), None, "tensor"),
            P(None, "tensor"),
            P("tensor"),
            P("tensor"),
            P(None, "tensor"),
            P("tensor"),
            P("tensor", "expert"),
            P(("groups", "expert"), None),
            P(),
            P(("groups", "expert"), None),
            P(("groups", "expert"), None),
            P(("expert", "tensor"), None),
            P(("expert", "tensor"), None),
            P(("expert", "tensor"), None),
        ),
        out_specs=(P(("groups", "expert"), None), P(("groups", "expert"), None, "tensor")),
        check_vma=False,
    )
```

profile of v0, /device:TPU:0, one launch (start us, length us, event | category | flops | bytes accessed | tf_op | source)
XLA Modules:
  0.0 134.9 jit_solution(396333789273066836)
XLA Ops:
  0.7 0.8 copy.73
  1.4 0.8 copy.71
  2.2 1.1 fusion.39
  3.3 1.0 exponential_negate_fusion
  4.3 0.7 broadcast_subtract_fusion
  4.9 1.0 fusion.32
  6.0 0.9 fusion.37
  6.9 1.1 fusion.38
  8.0 0.8 fusion.24
  8.8 32.3 %all-gather = bf16[8,2,4096]{2,1,0:T(2,128)(2,1)S(1)} all-gather(bf16[1,2,4096]{2,1,0:T(2,128)(2,1)S(1)} %fusion.24), channel_id=1, replica_groups=mesh['groups'=2,'expert'=8,'tensor'=2] {'expert'}, dimensions={0}, use_global_device_ids=true | all-gather | bytes 147456 | tf_op jit(solution)/shard_map/all_gather | solution.py:106
  41.2 2.8 %fusion.40 = f32[16,512]{1,0:T(8,128)S(1)} fusion(bf16[16,4096]{1,0:T(8,128)(2,1)S(1)} %reshape.106, bf16[4096,512]{1,0:T(8,128)(2,1)} %param.34), kind=kOutput, calls=%fused_computation.76 | convolution fusion | flops 67108864 | bytes 4358144 | tf_op jit(solution)/shard_map/dot_general | solution.py:105
  44.0 0.7 all_to_all.23
  44.7 5.5 %all-to-all-start = ((f32[8,2,512]{2,1,0:T(2,128)}), f32[8,2,512]{2,1,0:T(2,128)S(1)}, u32[]{:S(2)}, u32[]{:S(2)}) async-start(f32[8,2,512]{2,1,0:T(2,128)} %all_to_all.23), calls=%async_computation | async-start | bytes 65536 | tf_op jit(solution)/shard_map/all_to_all | solution.py:110
  50.1 0.7 convert_element_type.85
  50.8 0.8 convert_reduce_fusion
  51.9 5.0 %all-to-all-done = f32[8,2,512]{2,1,0:T(2,128)S(1)} async-done(((f32[8,2,512]{2,1,0:T(2,128)}), f32[8,2,512]{2,1,0:T(2,128)S(1)}, u32[]{:S(2)}, u32[]{:S(2)}) %all-to-all-start) | async-done | bytes 32800 | tf_op jit(solution)/shard_map/all_to_all | solution.py:110
  57.4 3.3 %all-to-all-start.1 = ((bf16[8,2,3]{2,1,0:T(2,128)(2,1)}), bf16[8,2,3]{2,1,0:T(2,128)(2,1)S(1)}, u32[]{:S(2)}, u32[]{:S(2)}) async-start(bf16[8,2,3]{2,1,0:T(2,128)(2,1)} %broadcast_in_dim.29), calls=%async_computation.1 | async-start | bytes 8192 | tf_op jit(solution)/shard_map/all_to_all | solution.py:137
  60.7 3.4 %psum.14 = bf16[2,4096]{1,0:T(2,128)(2,1)S(1)} all-reduce(f32[2,4096]{1,0:T(2,128)S(1)} %bitcast.56), channel_id=1, replica_groups=mesh['groups'=2,'expert'=8,'tensor'=2] {'tensor'}, use_global_device_ids=true, to_apply=%region_1.2 | all-reduce | flops 8192 | bytes 49152 | tf_op jit(solution)/shard_map/psum | solution.py:111
  64.1 0.9 fusion.13
  65.0 0.8 fusion.15
  65.8 0.8 broadcast_select_fusion
  67.1 5.5 %all-to-all-start.2 = ((bf16[8,2,4096]{2,1,0:T(2,128)(2,1)}), bf16[8,2,4096]{2,1,0:T(2,128)(2,1)S(1)}, u32[]{:S(2)}, u32[]{:S(2)}) async-start(bf16[8,2,4096]{2,1,0:T(2,128)(2,1)} %broadcast_select_fusion), calls=%async_computation.2 | async-start | bytes 262144 | tf_op jit(solution)/shard_map/all_to_all | solution.py:136
  73.1 6.9 %all-to-all-done.2 = bf16[8,2,4096]{2,1,0:T(2,128)(2,1)S(1)} async-done(((bf16[8,2,4096]{2,1,0:T(2,128)(2,1)}), bf16[8,2,4096]{2,1,0:T(2,128)(2,1)S(1)}, u32[]{:S(2)}, u32[]{:S(2)}) %all-to-all-start.2) | async-done | bytes 131104 | tf_op jit(solution)/shard_map/all_to_all | solution.py:136
  80.1 11.3 %fusion.41 = f32[16,2304]{1,0:T(8,128)S(1)} fusion(bf16[16,4096]{1,0:T(8,128)(2,1)S(1)} %reshape.103, bf16[2304,4096]{1,0:T(8,128)(2,1)} %param.39), kind=kOutput, calls=%fused_computation.77 | convolution fusion | flops 301989888 | bytes 19152896 | tf_op jit(solution)/shard_map/dot_general | solution.py:40
  91.5 11.3 %fusion.2 = bf16[16,2304]{1,0:T(8,128)(2,1)S(1)} fusion(bf16[16,4096]{1,0:T(8,128)(2,1)S(1)} %reshape.103, bf16[2304,4096]{1,0:T(8,128)(2,1)} %param.40, f32[16,2304]{1,0:T(8,128)S(1)} %fusion.41), kind=kOutput, calls=%fused_computation.6 | convolution fusion | flops 302211072 | bytes 19226624 | tf_op jit(solution)/shard_map/dot_general | solution.py:41
  102.8 7.7 %convolution_multiply_fusion.2 = f32[16,4096]{1,0:T(8,128)S(1)} fusion(bf16[2304,4096]{1,0:T(8,128)(2,1)} %param.41, f32[16]{0:T(128)S(1)} %mul.245, bf16[16,2304]{1,0:T(8,128)(2,1)S(1)} %fusion.2, pred[2304]{0:T(1024)(128)(4,1)S(1)} %get-tuple-element.38), kind=kOutput, calls=%fused_computation.4 | convolution fusion | flops 302092288 | bytes 19212608 | tf_op jit(solution)/shard_map/dot_general | solution.py:56
  110.5 7.7 %fusion.1 = f32[16,4096]{1,0:T(8,128)S(1)} fusion(f32[16,4096]{1,0:T(8,128)S(1)} %convolution_multiply_fusion.2, bf16[2304,4096]{1,0:T(8,128)(2,1)} %param.41, f32[16]{0:T(128)S(1)} %mul.262, bf16[16,2304]{1,0:T(8,128)(2,1)S(1)} %fusion.2, pred[2304]{0:T(1024)(128)(4,1)S(1)} %get-tuple-element.37), kind=kOutput, calls=%fused_computation.3 | convolution fusion | flops 302157824 | bytes 19474752 | tf_op jit(solution)/shard_map/dot_general | solution.py:57
  118.2 0.8 reshape.104
  119.1 3.4 %all-to-all-start.3 = ((f32[8,2,4096]{2,1,0:T(2,128)}), f32[8,2,4096]{2,1,0:T(2,128)S(1)}, u32[]{:S(2)}, u32[]{:S(2)}) async-start(f32[8,2,4096]{2,1,0:T(2,128)} %reshape.104), calls=%async_computation.3 | async-start | bytes 524288 | tf_op jit(solution)/shard_map/all_to_all | solution.py:142
  122.5 0.9 copy.79
  123.3 7.4 %all-to-all-done.3 = f32[8,2,4096]{2,1,0:T(2,128)S(1)} async-done(((f32[8,2,4096]{2,1,0:T(2,128)}), f32[8,2,4096]{2,1,0:T(2,128)S(1)}, u32[]{:S(2)}, u32[]{:S(2)}) %all-to-all-start.3) | async-done | bytes 262176 | tf_op jit(solution)/shard_map/all_to_all | solution.py:142
  130.9 3.4 %psum.15 = f32[2,4096]{1,0:T(2,128)S(1)} all-reduce(f32[2,4096]{1,0:T(2,128)S(1)} %reduce_sum.69), channel_id=1, replica_groups=mesh['groups'=2,'expert'=8,'tensor'=2] {'tensor'}, use_global_device_ids=true, to_apply=%region_8.9 | all-reduce | flops 8192 | bytes 65536 | tf_op jit(solution)/shard_map/psum | solution.py:143
  (21 shorter events, 2.7 us)
Async XLA Ops:
  0.6 6.3 %copy-start = (bf16[2,16,4096]{2,1,0:T(8,128)(2,1)S(1)}, bf16[2,16,4096]{2,1,0:T(8,128)(2,1)}, u32[]{:S(2)}) copy-start(bf16[2,16,4096]{2,1,0:T(8,128)(2,1)} %param.27) | copy-start | bytes 786436
  44.7 12.2 %all-to-all-start = ((f32[8,2,512]{2,1,0:T(2,128)}), f32[8,2,512]{2,1,0:T(2,128)S(1)}, u32[]{:S(2)}, u32[]{:S(2)}) async-start(f32[8,2,512]{2,1,0:T(2,128)} %all_to_all.23), calls=%async_computation | async-start | bytes 65536 | tf_op jit(solution)/shard_map/all_to_all | solution.py:110
  57.4 9.6 %all-to-all-start.1 = ((bf16[8,2,3]{2,1,0:T(2,128)(2,1)}), bf16[8,2,3]{2,1,0:T(2,128)(2,1)S(1)}, u32[]{:S(2)}, u32[]{:S(2)}) async-start(bf16[8,2,3]{2,1,0:T(2,128)(2,1)} %broadcast_in_dim.29), calls=%async_computation.1 | async-start | bytes 8192 | tf_op jit(solution)/shard_map/all_to_all | solution.py:137
  67.1 13.0 %all-to-all-start.2 = ((bf16[8,2,4096]{2,1,0:T(2,128)(2,1)}), bf16[8,2,4096]{2,1,0:T(2,128)(2,1)S(1)}, u32[]{:S(2)}, u32[]{:S(2)}) async-start(bf16[8,2,4096]{2,1,0:T(2,128)(2,1)} %broadcast_select_fusion), calls=%async_computation.2 | async-start | bytes 262144 | tf_op jit(solution)/shard_map/all_to_all | solution.py:136
  119.1 11.7 %all-to-all-start.3 = ((f32[8,2,4096]{2,1,0:T(2,128)}), f32[8,2,4096]{2,1,0:T(2,128)S(1)}, u32[]{:S(2)}, u32[]{:S(2)}) async-start(f32[8,2,4096]{2,1,0:T(2,128)} %reshape.104), calls=%async_computation.3 | async-start | bytes 524288 | tf_op jit(solution)/shard_map/all_to_all | solution.py:142
where the time goes:
time: 136 us; the launch traced here: 135 us
  matrix products  43.3 us (32%)
  blocking collectives  39.1 us (29%)
  waiting for transfers between devices  19.7 us (14%)
  starting transfers between devices  17.7 us (13%)
  other arithmetic  8.12 us (6%)
  local copies, waits for them, and re-layouts  6.19 us (5%)
    all_gather x1, blocking collectives, local(): lax.all_gather(gated_out, 'expert', axis=0, tiled=True)  32.3 us
    dot_general x1, matrix products, expert_terms(): lax.dot_general(rows, up_weight, dims, preferred_element_type=jnp.float32)  11.3 us
    dot_general x1, matrix products, expert_terms(): lax.dot_general(rows, gate_weight, dims, preferred_element_type=jnp.float32)  11.3 us
    dot_general x1, matrix products, expert_terms(): jnp.dot(lower_hidden, down_weight, preferred_element_type=jnp.float32)  7.7 us
    dot_general x1, matrix products, expert_terms(): jnp.dot(upper_hidden, down_weight, preferred_element_type=jnp.float32)  7.7 us
    all_to_all x1, waiting for transfers between devices, local(): lax.all_to_all(partial_value, 'expert', split_axis=0, concat_axis=0, tile...  7.44 us
    all_to_all x1, waiting for transfers between devices, local(): lax.all_to_all(outgoing, 'expert', split_axis=0, concat_axis=0, tiled=True)  6.94 us
    all_to_all x1, starting transfers between devices, local(): lax.all_to_all(outgoing, 'expert', split_axis=0, concat_axis=0, tiled=True)  5.52 us
  transfers between devices with their start and end apart: 4, of which 4 were waited for; matrix products, arithmetic and copies ran while one was open for 4% of the time, Pallas kernels for 0%

commit v1 on v0

--- a/solution.py
+++ b/solution.py
@@ -1,6 +1,8 @@
 import jax
 import jax.numpy as jnp
 from jax import lax
+from jax.experimental import pallas as pl
+from jax.experimental.pallas import tpu as pltpu
 from jax.sharding import PartitionSpec as P
 
 EXPERTS = 3
@@ -145,9 +147,328 @@
     return (layer_out, state_next.astype(jnp.bfloat16))
 
 
+LANES = 128
+BLOCK = 256
+EPS = 1e-05
+VMEM = pl.BlockSpec(memory_space=pltpu.VMEM)
+SMEM = pl.BlockSpec(memory_space=pltpu.SMEM)
+ANY = pl.BlockSpec(memory_space=pl.ANY)
+F32 = jnp.float32
+BF16 = jnp.bfloat16
+
+
+def lane_to_sublane(row):
+    n = row.shape[1]
+    spread = jnp.broadcast_to(row, (n, n))
+    diagonal = lax.broadcasted_iota(jnp.int32, (n, n), 0) == lax.broadcasted_iota(
+        jnp.int32, (n, n), 1
+    )
+    return jnp.sum(jnp.where(diagonal, spread, 0.0), axis=1, keepdims=True)
+
+
+def mixer_kernel(
+    slot_ref,
+    ids_ref,
+    conv_input,
+    gate_input,
+    step_input,
+    b_proj,
+    c_proj,
+    state_pool,
+    conv_pool,
+    conv_weight,
+    conv_bias,
+    step_bias,
+    a_log,
+    d_skip,
+    residual,
+    probs,
+    new_state,
+    packet,
+):
+    rows, channels = conv_input.shape
+    peers = packet.shape[0]
+    cols = residual.shape[1] // peers
+    first_slot = lax.axis_index("expert") * state_pool.shape[0]
+    rates = -jnp.exp(a_log[...])
+    lane = lax.broadcasted_iota(jnp.int32, (1, LANES), 1)
+    for r in range(rows):
+        slot = slot_ref[r] - first_slot
+        conv = conv_weight[-1:, :] * conv_input[r : r + 1, :].astype(F32) + conv_bias[...]
+        for lag in range(conv_pool.shape[0]):
+            past = conv_pool[lag].astype(F32)
+            picked = lax.broadcasted_iota(jnp.int32, past.shape, 0) == slot
+            history = jnp.sum(jnp.where(picked, past, 0.0), axis=0, keepdims=True)
+            conv = conv + conv_weight[lag : lag + 1, :] * history
+        conv_out = conv * jax.nn.sigmoid(conv)
+        step = jax.nn.softplus(step_input[r : r + 1, :].astype(F32) + step_bias[...])
+        b = lane_to_sublane(b_proj[r : r + 1, :])
+        c = lane_to_sublane(c_proj[r : r + 1, :])
+        state = jnp.exp(step * rates) * state_pool[slot].astype(F32) + (step * conv_out) * b
+        new_state[r] = state.astype(BF16)
+        output = jnp.sum(c * state, axis=0, keepdims=True) + d_skip[...] * conv_out
+        gate = gate_input[r : r + 1, :].astype(F32)
+        gated = (output * (gate * jax.nn.sigmoid(gate))).astype(BF16)
+        coefs = jnp.zeros((1, LANES), F32)
+        for k in range(ids_ref.shape[1]):
+            coefs = coefs + jnp.where(lane == ids_ref[r, k], probs[r, k], 0.0)
+        coefs = coefs.astype(BF16)
+        for d in range(peers):
+            packet[d, r : r + 1, 0:channels] = gated
+            packet[d, r : r + 1, channels : channels + cols] = residual[
+                r : r + 1, d * cols : (d + 1) * cols
+            ]
+            packet[d, r : r + 1, channels + cols :] = coefs
+
+
+def project_kernel(packets, out_weight, partial, residual_block, coefs, rows_scratch):
+    peers, rows, _ = packets.shape
+    channels, cols = out_weight.shape
+    for d in range(peers):
+        rows_scratch[d * rows : (d + 1) * rows, :] = packets[d].astype(F32)
+    partial[...] = jnp.dot(
+        rows_scratch[:, 0:channels].astype(BF16), out_weight[...], preferred_element_type=F32
+    )
+    residual_block[...] = rows_scratch[:, channels : channels + cols]
+    coefs[...] = rows_scratch[:, channels + cols :]
+
+
+def hidden_kernel(mine, other, residual_block, copies):
+    mixed = (mine[...] + other[...]).astype(BF16).astype(F32)
+    hidden = (residual_block[...] + mixed).astype(BF16)
+    for d in range(copies.shape[0]):
+        copies[d] = hidden
+
+
+def expert_kernel(
+    hidden,
+    coefs,
+    gain,
+    gate_hbm,
+    up_hbm,
+    down_hbm,
+    partial,
+    own_rows,
+    gate_buf,
+    up_buf,
+    down_buf,
+    wide,
+    normed,
+    units_out,
+    total,
+    gate_sem,
+    up_sem,
+    down_sem,
+):
+    units, width = gate_buf.shape
+    peers, rows, cols = hidden.shape
+    blocks = units // BLOCK
+
+    def copy_of(weight, buffer, sem, i):
+        part = pl.ds(i * BLOCK, BLOCK)
+        return pltpu.make_async_copy(weight.at[part], buffer.at[part], sem.at[i])
+
+    for i in range(blocks):
+        copy_of(gate_hbm, gate_buf, gate_sem, i).start()
+        copy_of(up_hbm, up_buf, up_sem, i).start()
+    for i in range(blocks):
+        copy_of(down_hbm, down_buf, down_sem, i).start()
+
+    for d in range(peers):
+        wide[:, d * cols : (d + 1) * cols] = hidden[d].astype(F32)
+    mean = jnp.sum(wide[...] * wide[...], axis=1, keepdims=True) * (1.0 / width)
+    normed[...] = (wide[...] * lax.rsqrt(mean + EPS) * gain[...]).astype(BF16)
+    expert = lax.axis_index("expert")
+    own = own_rows.shape[0]
+    mine = wide[0:own, :]
+    for d in range(1, peers):
+        mine = jnp.where(expert == d, wide[d * own : (d + 1) * own, :], mine)
+    own_rows[...] = mine
+
+    first_unit = (expert * lax.axis_size("tensor") + lax.axis_index("tensor")) * units
+    lower = first_unit // FF
+    boundary = (lower + 1) * FF - first_unit
+    lane = lax.broadcasted_iota(jnp.int32, coefs.shape, 1)
+    lower_coef = jnp.sum(jnp.where(lane == lower, coefs[...], 0.0), axis=1, keepdims=True)
+    upper_coef = jnp.sum(jnp.where(lane == lower + 1, coefs[...], 0.0), axis=1, keepdims=True)
+    dims = (((1,), (1,)), ((), ()))
+
+    def unit_block(i, carry):
+        copy_of(gate_hbm, gate_buf, gate_sem, i).wait()
+        copy_of(up_hbm, up_buf, up_sem, i).wait()
+        start = pl.multiple_of(i * BLOCK, BLOCK)
+        part = pl.ds(start, BLOCK)
+        gate = lax.dot_general(normed[...], gate_buf[part, :], dims, preferred_element_type=F32)
+        up = lax.dot_general(normed[...], up_buf[part, :], dims, preferred_element_type=F32)
+        column = lax.broadcasted_iota(jnp.int32, (rows, BLOCK), 1) + start
+        coef = jnp.where(column < boundary, lower_coef, upper_coef)
+        units_out[:, part] = (gate * jax.nn.sigmoid(gate) * up * coef).astype(BF16)
+        return carry
+
+    lax.fori_loop(0, blocks, unit_block, 0)
+    total[...] = jnp.zeros_like(total)
+
+    def down_block(i, carry):
+        copy_of(down_hbm, down_buf, down_sem, i).wait()
+        part = pl.ds(pl.multiple_of(i * BLOCK, BLOCK), BLOCK)
+        total[...] += jnp.dot(units_out[:, part], down_buf[part, :], preferred_element_type=F32)
+        return carry
+
+    lax.fori_loop(0, blocks, down_block, 0)
+    pieces, piece_rows, piece_cols = partial.shape
+    across = width // piece_cols
+    for p in range(pieces):
+        r, c = p // across, p % across
+        partial[p] = total[
+            r * piece_rows : (r + 1) * piece_rows, c * piece_cols : (c + 1) * piece_cols
+        ]
+
+
+def sum_kernel(pieces, own_rows, out):
+    half = out.shape[1]
+    total = jnp.sum(pieces[...], axis=0)
+    start = pl.multiple_of(lax.axis_index("tensor") * half, half)
+    out[...] = (own_rows[:, pl.ds(start, half)] + total).astype(BF16)
+
+
+def fused(
+    conv_input,
+    gate_input,
+    step_input,
+    b_proj,
+    c_proj,
+    slot_ids,
+    state_pool,
+    conv_pool,
+    conv_weight,
+    conv_bias,
+    step_bias,
+    a_log,
+    d_skip,
+    out_weight,
+    residual,
+    norm_gain,
+    expert_ids,
+    expert_probs,
+    gate_weight,
+    up_weight,
+    down_weight,
+):
+    rows, channels = conv_input.shape
+    width = residual.shape[1]
+    units = gate_weight.shape[0]
+    cols = out_weight.shape[1]
+    peers = lax.axis_size("expert")
+    halves = lax.axis_size("tensor")
+    all_rows = peers * rows
+    shape = jax.ShapeDtypeStruct
+    packet_width = channels + cols + LANES
+
+    new_state, packet = pl.pallas_call(
+        mixer_kernel,
+        out_shape=(
+            shape((rows,) + state_pool.shape[1:], BF16),
+            shape((peers, rows, packet_width), BF16),
+        ),
+        in_specs=[SMEM, SMEM] + [VMEM] * 13 + [SMEM],
+        out_specs=(VMEM, VMEM),
+        name="mixer",
+    )(
+        slot_ids,
+        expert_ids,
+        conv_input,
+        gate_input,
+        step_input,
+        b_proj,
+        c_proj,
+        state_pool,
+        jnp.transpose(conv_pool, (1, 0, 2)),
+        conv_weight,
+        conv_bias[None],
+        step_bias[None],
+        a_log,
+        d_skip[None],
+        residual,
+        expert_probs.astype(F32),
+    )
+    packets = lax.all_to_all(packet, "expert", split_axis=0, concat_axis=0, tiled=True)
+    partial_mixed, residual_block, coefs = pl.pallas_call(
+        project_kernel,
+        out_shape=(
+            shape((all_rows, cols), F32),
+            shape((all_rows, cols), F32),
+            shape((all_rows, LANES), F32),
+        ),
+        in_specs=[VMEM] * 2,
+        out_specs=(VMEM,) * 3,
+        scratch_shapes=[pltpu.VMEM((all_rows, packet_width), F32)],
+        name="project",
+    )(packets, out_weight)
+    swap = [(i, halves - 1 - i) for i in range(halves)]
+    other_mixed = lax.ppermute(partial_mixed, "tensor", swap)
+    hidden_copies = pl.pallas_call(
+        hidden_kernel,
+        out_shape=shape((peers, all_rows, cols), BF16),
+        in_specs=[VMEM] * 3,
+        out_specs=VMEM,
+        name="hidden",
+    )(partial_mixed, other_mixed, residual_block)
+    hidden = lax.all_to_all(hidden_copies, "expert", split_axis=0, concat_axis=0, tiled=True)
+    blocks = units // BLOCK
+    partial_out, own_rows = pl.pallas_call(
+        expert_kernel,
+        out_shape=(
+            shape((peers * halves, rows, width // halves), F32),
+            shape((rows, width), F32),
+        ),
+        in_specs=[VMEM] * 3 + [ANY] * 3,
+        out_specs=(VMEM, VMEM),
+        scratch_shapes=[
+            pltpu.VMEM((units, width), BF16),
+            pltpu.VMEM((units, width), BF16),
+            pltpu.VMEM((units, width), BF16),
+            pltpu.VMEM((all_rows, width), F32),
+            pltpu.VMEM((all_rows, width), BF16),
+            pltpu.VMEM((all_rows, units), BF16),
+            pltpu.VMEM((all_rows, width), F32),
+            pltpu.SemaphoreType.DMA((blocks,)),
+            pltpu.SemaphoreType.DMA((blocks,)),
+            pltpu.SemaphoreType.DMA((blocks,)),
+        ],
+        compiler_params=pltpu.CompilerParams(vmem_limit_bytes=60 * 2**20),
+        name="experts",
+    )(hidden, coefs, norm_gain[None], gate_weight, up_weight, down_weight)
+    pieces = lax.all_to_all(
+        partial_out, ("expert", "tensor"), split_axis=0, concat_axis=0, tiled=True
+    )
+    half_out = pl.pallas_call(
+        sum_kernel,
+        out_shape=shape((rows, width // halves), BF16),
+        in_specs=[VMEM] * 2,
+        out_specs=VMEM,
+        name="sum",
+    )(pieces, own_rows)
+    other_half = lax.ppermute(half_out, "tensor", swap)
+    first = lax.axis_index("tensor") == 0
+    layer_out = jnp.concatenate(
+        [jnp.where(first, half_out, other_half), jnp.where(first, other_half, half_out)], axis=1
+    )
+    return (layer_out, new_state)
+
+
+def body(*args):
+    out_weight, gate_weight = args[13], args[18]
+    tiled = (
+        out_weight.shape[1] % LANES == 0
+        and gate_weight.shape[0] % BLOCK == 0
+        and lax.axis_size("tensor") == 2
+    )
+    return fused(*args) if tiled else local(*args)
+
+
 def solution(mesh):
     return jax.shard_map(
-        local,
+        body,
         mesh=mesh,
         in_specs=(
             P(("groups", "expert"), "tensor"),

time: 136 us -> 80.5 us (0.59)
  matrix products: 43.3 us -> 0 us
  Pallas kernels: 0 us -> 32.6 us
  starting transfers between devices: 17.7 us -> 0.01 us
  waiting for transfers between devices: 19.7 us -> 2.8 us
  local copies, waits for them, and re-layouts: 6.19 us -> 0.61 us
  other arithmetic: 8.12 us -> 2.56 us
  blocking collectives: 39.1 us -> 40.6 us
    dot_general x8 -> x0, matrix products: 43.3 us -> none  [the longest x1 11.3 us: expert_terms(): lax.dot_general(rows, up_weight, dims, preferred_element_type=jnp.float32)]
    all_to_all x0 -> x3, blocking collectives: none -> 40.6 us  [the longest x1 14.8 us: fused(): lax.all_to_all(packet, 'expert', split_axis=0, concat_axis=0, tiled=True)]
    pallas_call x0 -> x5, Pallas kernels: none -> 32.6 us  [the longest x1 23.3 us: fused(): pl.pallas_call(expert_kernel, out_shape=(shape((peers * halves, rows, wid...]
    all_gather x1 -> x0, blocking collectives: 32.3 us -> none  [local(): lax.all_gather(gated_out, 'expert', axis=0, tiled=True)]
    all_to_all x4 -> x0, waiting for transfers between devices: 19.7 us -> none  [the longest x1 7.44 us: local(): lax.all_to_all(partial_value, 'expert', split_axis=0, concat_axis=0, tile...]
    all_to_all x4 -> x0, starting transfers between devices: 17.7 us -> none  [the longest x1 5.52 us: local(): lax.all_to_all(outgoing, 'expert', split_axis=0, concat_axis=0, tiled=True)]
    psum x2 -> x0, blocking collectives: 6.81 us -> none  [the longest x1 3.41 us: local(): mixed = lax.psum(returned_cols, 'tensor').astype(jnp.bfloat16)]
    ppermute x0 -> x2, waiting for transfers between devices: none -> 2.8 us  [the longest x1 1.42 us: fused(): other_mixed = lax.ppermute(partial_mixed, 'tensor', swap)]
  transfers between devices with their start and end apart: 4 -> 2, of which waited for: 4 -> 2; matrix products, arithmetic and copies ran while one was open for 4% -> 0% of each run, Pallas kernels for 0% -> 0%
where the time goes in v1:
time: 80.5 us; the launch traced here: 79.9 us
  blocking collectives  40.6 us (50%)
  Pallas kernels  32.6 us (40%)
  waiting for transfers between devices  2.8 us (3%)
  other arithmetic  2.56 us (3%)
    pallas_call x1, Pallas kernels, fused(): pl.pallas_call(expert_kernel, out_shape=(shape((peers * halves, rows, wid...  23.3 us
    all_to_all x1, blocking collectives, fused(): lax.all_to_all(packet, 'expert', split_axis=0, concat_axis=0, tiled=True)  14.8 us
    all_to_all x1, blocking collectives, fused(): lax.all_to_all(partial_out, ('expert', 'tensor'), split_axis=0, concat_ax...  14.2 us
    all_to_all x1, blocking collectives, fused(): lax.all_to_all(hidden_copies, 'expert', split_axis=0, concat_axis=0, tile...  11.6 us
    pallas_call x1, Pallas kernels, fused(): pl.pallas_call(project_kernel, out_shape=(shape((all_rows, cols), F32), s...  3.55 us
    pallas_call x1, Pallas kernels, fused(): pl.pallas_call(mixer_kernel, out_shape=(shape((rows,) + state_pool.shape[...  2.65 us
    pallas_call x1, Pallas kernels, fused(): pl.pallas_call(sum_kernel, out_shape=shape((rows, width // halves), BF16)...  1.68 us
  transfers between devices with their start and end apart: 2, of which 2 were waited for; matrix products, arithmetic and copies ran while one was open for 0% of the time, Pallas kernels for 0%

profile of v1, /device:TPU:0, one launch (start us, length us, event | category | flops | bytes accessed | tf_op | source)
XLA Modules:
  0.0 79.9 jit_solution(11253988847416467629)
XLA Ops:
  0.6 1.2 %convert_element_type.3.probs = f32[2,2]{1,0:T(2,128)} convert(bf16[2,2]{1,0:T(2,128)(2,1)} %param.38) | non-fusion elementwise | flops 4 | bytes 24 | tf_op jit(solution)/shard_map/convert_element_type | solution.py:392
  1.8 2.7 %mixer.1 = (bf16[2,16,4096]{2,1,0:T(8,128)(2,1)}, bf16[8,2,4736]{2,1,0:T(2,128)(2,1)}) custom-call(s32[2]{0:T(128)} %slot_ref.1, s32[2,2]{1,0:T(2,128)} %ids_ref.1, bf16[2,4096]{1,0:T(2,128)(2,1)} %conv_input.1, bf16[2,4096]{1,0:T(2,128)(2,1)} %gate_input.1, bf16[2,4096]{1,0:T(2,128)(2,1)} %step_input.1, f32[2,16]{1,0:T(2,128)} %b_proj.1, f32[2,16]{1,0:T(2,128)} %c_proj.1, ...), custom_call_target="tpu_custom_call" | custom-call | tf_op jit(solution)/shard_map/mixer/pallas_call | solution.py:367
  4.5 14.8 %all_to_all.15.packets = bf16[8,2,4736]{2,1,0:T(2,128)(2,1)} all-to-all(bf16[8,2,4736]{2,1,0:T(2,128)(2,1)} %get-tuple-element.9), channel_id=1, replica_groups=mesh['groups'=2,'expert'=8,'tensor'=2] {'expert'}, dimensions={0} | all-to-all | bytes 303104 | tf_op jit(solution)/shard_map/all_to_all | solution.py:394
  19.3 3.5 %project.1 = (f32[16,512]{1,0:T(8,128)}, f32[16,512]{1,0:T(8,128)}, f32[16,128]{1,0:T(8,128)}) custom-call(bf16[8,2,4736]{2,1,0:T(2,128)(2,1)} %all_to_all.15.packets, bf16[4096,512]{1,0:T(8,128)(2,1)} %out_weight.1), custom_call_target="tpu_custom_call" | custom-call | tf_op jit(solution)/shard_map/project/pallas_call | solution.py:395
  22.9 0.0 collective-permute-start
  22.9 1.4 %collective-permute-done.other = f32[16,512]{1,0:T(8,128)S(1)} collective-permute-done((f32[16,512]{1,0:T(8,128)}, f32[16,512]{1,0:T(8,128)S(1)}, u32[]{:S(2)}, u32[]{:S(2)}) %collective-permute-start) | collective-permute-done | bytes 32800 | tf_op jit(solution)/shard_map/ppermute | solution.py:408
  24.3 0.0 copy-start
  24.3 0.6 copy-done
  24.9 1.5 %hidden.1 = bf16[8,16,512]{2,1,0:T(8,128)(2,1)} custom-call(f32[16,512]{1,0:T(8,128)} %get-tuple-element.10.mine, f32[16,512]{1,0:T(8,128)} %copy-done, f32[16,512]{1,0:T(8,128)} %get-tuple-element.11.residual_block), custom_call_target="tpu_custom_call" | custom-call | tf_op jit(solution)/shard_map/hidden/pallas_call | solution.py:409
  26.4 11.6 %all_to_all.16.hidden = bf16[8,16,512]{2,1,0:T(8,128)(2,1)} all-to-all(bf16[8,16,512]{2,1,0:T(8,128)(2,1)} %hidden.1), channel_id=1, replica_groups=mesh['groups'=2,'expert'=8,'tensor'=2] {'expert'}, dimensions={0} | all-to-all | bytes 262144 | tf_op jit(solution)/shard_map/all_to_all | solution.py:416
  37.9 23.3 %experts.1 = (f32[16,2,2048]{2,1,0:T(2,128)}, f32[2,4096]{1,0:T(2,128)}) custom-call(bf16[8,16,512]{2,1,0:T(8,128)(2,1)} %all_to_all.16.hidden, f32[16,128]{1,0:T(8,128)} %get-tuple-element.12.coefs, f32[1,4096]{1,0:T(1,128)} %bitcast.6, bf16[2304,4096]{1,0:T(8,128)(2,1)} %gate_hbm.1, bf16[2304,4096]{1,0:T(8,128)(2,1)} %up_hbm.1, bf16[2304,4096]{1,0:T(8,128)(2,1)} %down_hbm.1), custom_call_target="tpu_custom_call" | custom-call | tf_op jit(solution)/shard_map/experts/pallas_call | solution.py:418
  61.2 14.2 %all_to_all.17.pieces = f32[16,2,2048]{2,1,0:T(2,128)} all-to-all(f32[16,2,2048]{2,1,0:T(2,128)} %get-tuple-element.13), channel_id=1, replica_groups=mesh['groups'=2,'expert'=8,'tensor'=2] {'expert','tensor'}, dimensions={0} | all-to-all | bytes 524288 | tf_op jit(solution)/shard_map/all_to_all | solution.py:441
  75.5 1.7 %sum.1 = bf16[2,2048]{1,0:T(2,128)(2,1)} custom-call(f32[16,2,2048]{2,1,0:T(2,128)} %all_to_all.17.pieces, f32[2,4096]{1,0:T(2,128)} %get-tuple-element.14.own_rows), custom_call_target="tpu_custom_call" | custom-call | tf_op jit(solution)/shard_map/sum/pallas_call | solution.py:444
  77.2 0.0 collective-permute-start.1
  77.2 1.4 %collective-permute-done.1 = bf16[2,2048]{1,0:T(2,128)(2,1)S(1)} collective-permute-done((bf16[2,2048]{1,0:T(2,128)(2,1)}, bf16[2,2048]{1,0:T(2,128)(2,1)S(1)}, u32[]{:S(2)}, u32[]{:S(2)}) %collective-permute-start.1) | collective-permute-done | bytes 8224 | tf_op jit(solution)/shard_map/ppermute | solution.py:451
  78.6 0.7 broadcast_select_fusion.1
  79.3 0.6 pad_maximum_fusion
Async XLA Ops:
  22.9 1.4 %collective-permute-start = (f32[16,512]{1,0:T(8,128)}, f32[16,512]{1,0:T(8,128)S(1)}, u32[]{:S(2)}, u32[]{:S(2)}) collective-permute-start(f32[16,512]{1,0:T(8,128)} %get-tuple-element.10.mine), channel_id=1, source_target_pairs={{0,1},{1,0},{2,3},{3,2},{4,5},{5,4},{6,7},{7,6},{8,9},{9,8},{10,11... | collective-permute-start | bytes 98312 | tf_op jit(solution)/shard_map/ppermute | solution.py:408
  24.3 0.6 copy-start
  77.2 1.4 %collective-permute-start.1 = (bf16[2,2048]{1,0:T(2,128)(2,1)}, bf16[2,2048]{1,0:T(2,128)(2,1)S(1)}, u32[]{:S(2)}, u32[]{:S(2)}) collective-permute-start(bf16[2,2048]{1,0:T(2,128)(2,1)} %sum.1), channel_id=1, source_target_pairs={{0,1},{1,0},{2,3},{3,2},{4,5},{5,4},{6,7},{7,6},{8,9},{9,8},{10,11... | collective-permute-start | bytes 24584 | tf_op jit(solution)/shard_map/ppermute | solution.py:451

commit v2 on v1

--- a/solution.py
+++ b/solution.py
@@ -148,11 +148,19 @@
 
 
 LANES = 128
-BLOCK = 256
+BLOCK = 768
+CHUNK = 384
+SLOTS = 5
 EPS = 1e-05
 VMEM = pl.BlockSpec(memory_space=pltpu.VMEM)
 SMEM = pl.BlockSpec(memory_space=pltpu.SMEM)
 ANY = pl.BlockSpec(memory_space=pl.ANY)
+
+
+def beside(bytes_accessed):
+    return pl.CostEstimate(flops=bytes_accessed * 300, bytes_accessed=bytes_accessed, transcendentals=0)
+
+
 F32 = jnp.float32
 BF16 = jnp.bfloat16
 
@@ -166,52 +174,70 @@
     return jnp.sum(jnp.where(diagonal, spread, 0.0), axis=1, keepdims=True)
 
 
-def mixer_kernel(
-    slot_ref,
-    ids_ref,
-    conv_input,
-    gate_input,
-    step_input,
-    b_proj,
-    c_proj,
-    state_pool,
-    conv_pool,
-    conv_weight,
-    conv_bias,
-    step_bias,
-    a_log,
-    d_skip,
-    residual,
-    probs,
-    new_state,
-    packet,
-):
+def mixer_kernel(*refs):
+    sources, (new_state, packet) = refs[:16], refs[16:18]
+    buffers, sems = refs[18:34], refs[34]
+    copies = [
+        pltpu.make_async_copy(source, buffer, sems.at[i])
+        for i, (source, buffer) in enumerate(zip(sources, buffers))
+    ]
+    for copy in copies:
+        copy.start()
+    for copy in copies:
+        copy.wait()
+    (
+        slot_ref,
+        ids_ref,
+        conv_input,
+        gate_input,
+        step_input,
+        b_proj,
+        c_proj,
+        state_pool,
+        conv_pool,
+        conv_weight,
+        conv_bias,
+        step_bias,
+        a_log,
+        d_skip,
+        residual,
+        probs,
+    ) = buffers
     rows, channels = conv_input.shape
     peers = packet.shape[0]
     cols = residual.shape[1] // peers
     first_slot = lax.axis_index("expert") * state_pool.shape[0]
     rates = -jnp.exp(a_log[...])
     lane = lax.broadcasted_iota(jnp.int32, (1, LANES), 1)
+    row = lax.broadcasted_iota(jnp.int32, (rows, channels), 0)
+    slots = [slot_ref[r] - first_slot for r in range(rows)]
+    conv = conv_weight[-1:, :] * conv_input[...].astype(F32) + conv_bias[...]
+    for lag in range(conv_pool.shape[0]):
+        past = conv_pool[lag].astype(F32)
+        history = jnp.zeros((rows, channels), F32)
+        for r in range(rows):
+            for p in range(past.shape[0]):
+                taken = (row == r) & (slots[r] == p)
+                history = jnp.where(taken, past[p : p + 1, :], history)
+        conv = conv + conv_weight[lag : lag + 1, :] * history
+    conv_outs = conv * jax.nn.sigmoid(conv)
+    steps = jax.nn.softplus(step_input[...].astype(F32) + step_bias[...])
+    drives = steps * conv_outs
+    gates = gate_input[...].astype(F32)
+    gates = gates * jax.nn.sigmoid(gates)
+    skips = d_skip[...] * conv_outs
     for r in range(rows):
-        slot = slot_ref[r] - first_slot
-        conv = conv_weight[-1:, :] * conv_input[r : r + 1, :].astype(F32) + conv_bias[...]
-        for lag in range(conv_pool.shape[0]):
-            past = conv_pool[lag].astype(F32)
-            picked = lax.broadcasted_iota(jnp.int32, past.shape, 0) == slot
-            history = jnp.sum(jnp.where(picked, past, 0.0), axis=0, keepdims=True)
-            conv = conv + conv_weight[lag : lag + 1, :] * history
-        conv_out = conv * jax.nn.sigmoid(conv)
-        step = jax.nn.softplus(step_input[r : r + 1, :].astype(F32) + step_bias[...])
         b = lane_to_sublane(b_proj[r : r + 1, :])
         c = lane_to_sublane(c_proj[r : r + 1, :])
-        state = jnp.exp(step * rates) * state_pool[slot].astype(F32) + (step * conv_out) * b
+        past = state_pool[slots[r]].astype(F32)
+        state = jnp.exp(steps[r : r + 1, :] * rates) * past + drives[r : r + 1, :] * b
         new_state[r] = state.astype(BF16)
-        output = jnp.sum(c * state, axis=0, keepdims=True) + d_skip[...] * conv_out
-        gate = gate_input[r : r + 1, :].astype(F32)
-        gated = (output * (gate * jax.nn.sigmoid(gate))).astype(BF16)
+        output = jnp.sum(c * state, axis=0, keepdims=True) + skips[r : r + 1, :]
+        gated = (output * gates[r : r + 1, :]).astype(BF16)
         coefs = jnp.zeros((1, LANES), F32)
+        prob = probs[r : r + 1, :].astype(F32)
         for k in range(ids_ref.shape[1]):
-            coefs = coefs + jnp.where(lane == ids_ref[r, k], probs[r, k], 0.0)
+            coefs = coefs + jnp.where(lane == ids_ref[r, k], prob[:, k : k + 1], 0.0)
         coefs = coefs.astype(BF16)
         for d in range(peers):
             packet[d, r : r + 1, 0:channels] = gated
@@ -244,35 +270,35 @@
     hidden,
     coefs,
     gain,
-    gate_hbm,
-    up_hbm,
+    gate_weight,
+    up_weight,
     down_hbm,
     partial,
     own_rows,
-    gate_buf,
-    up_buf,
     down_buf,
     wide,
     normed,
     units_out,
     total,
-    gate_sem,
-    up_sem,
     down_sem,
 ):
-    units, width = gate_buf.shape
+    units, width = gate_weight.shape
     peers, rows, cols = hidden.shape
     blocks = units // BLOCK
 
-    def copy_of(weight, buffer, sem, i):
-        part = pl.ds(i * BLOCK, BLOCK)
-        return pltpu.make_async_copy(weight.at[part], buffer.at[part], sem.at[i])
-
-    for i in range(blocks):
-        copy_of(gate_hbm, gate_buf, gate_sem, i).start()
-        copy_of(up_hbm, up_buf, up_sem, i).start()
-    for i in range(blocks):
-        copy_of(down_hbm, down_buf, down_sem, i).start()
+    chunks = units // CHUNK
+    slots = down_buf.shape[0] // CHUNK
+
+    def down_copy(i):
+        slot = i % slots
+        return pltpu.make_async_copy(
+            down_hbm.at[pl.ds(i * CHUNK, CHUNK)],
+            down_buf.at[pl.ds(slot * CHUNK, CHUNK)],
+            down_sem.at[slot],
+        )
+
+    for i in range(slots):
+        down_copy(i).start()
 
     for d in range(peers):
         wide[:, d * cols : (d + 1) * cols] = hidden[d].astype(F32)
@@ -294,41 +320,78 @@
     dims = (((1,), (1,)), ((), ()))
 
     def unit_block(i, carry):
-        copy_of(gate_hbm, gate_buf, gate_sem, i).wait()
-        copy_of(up_hbm, up_buf, up_sem, i).wait()
         start = pl.multiple_of(i * BLOCK, BLOCK)
         part = pl.ds(start, BLOCK)
-        gate = lax.dot_general(normed[...], gate_buf[part, :], dims, preferred_element_type=F32)
-        up = lax.dot_general(normed[...], up_buf[part, :], dims, preferred_element_type=F32)
+        gate = lax.dot_general(normed[...], gate_weight[part, :], dims, preferred_element_type=F32)
+        up = lax.dot_general(normed[...], up_weight[part, :], dims, preferred_element_type=F32)
         column = lax.broadcasted_iota(jnp.int32, (rows, BLOCK), 1) + start
         coef = jnp.where(column < boundary, lower_coef, upper_coef)
         units_out[:, part] = (gate * jax.nn.sigmoid(gate) * up * coef).astype(BF16)
         return carry
 
     lax.fori_loop(0, blocks, unit_block, 0)
-    total[...] = jnp.zeros_like(total)
-
-    def down_block(i, carry):
-        copy_of(down_hbm, down_buf, down_sem, i).wait()
-        part = pl.ds(pl.multiple_of(i * BLOCK, BLOCK), BLOCK)
-        total[...] += jnp.dot(units_out[:, part], down_buf[part, :], preferred_element_type=F32)
-        return carry
-
-    lax.fori_loop(0, blocks, down_block, 0)
-    pieces, piece_rows, piece_cols = partial.shape
-    across = width // piece_cols
-    for p in range(pieces):
-        r, c = p // across, p % across
-        partial[p] = total[
-            r * piece_rows : (r + 1) * piece_rows, c * piece_cols : (c + 1) * piece_cols
-        ]
-
-
-def sum_kernel(pieces, own_rows, out):
-    half = out.shape[1]
-    total = jnp.sum(pieces[...], axis=0)
-    start = pl.multiple_of(lax.axis_index("tensor") * half, half)
-    out[...] = (own_rows[:, pl.ds(start, half)] + total).astype(BF16)
+    first = 0
+    while first < chunks:
+        slot = first % slots
+        count = min(BLOCK // CHUNK, chunks - first, slots - slot)
+        for i in range(first, first + count):
+            down_copy(i).wait()
+        product = jnp.dot(
+            units_out[:, first * CHUNK : (first + count) * CHUNK],
+            down_buf[slot * CHUNK : (slot + count) * CHUNK, :],
+            preferred_element_type=F32,
+        )
+        total[...] = product if first == 0 else total[...] + product
+        for i in range(first + slots, min(first + count + slots, chunks)):
+            down_copy(i).start()
+        first += count
+
+    for d in range(peers):
+        partial[d] = total[d * own : (d + 1) * own, :].astype(BF16)
+
+
+def sum_kernel(pieces, out):
+    total = pieces[0].astype(F32)
+    for d in range(1, pieces.shape[0]):
+        total = total + pieces[d].astype(F32)
+    out[...] = total
+
+
+def output_kernel(mine, other, own_rows, out):
+    out[...] = (own_rows[...] + (mine[...] + other[...])).astype(BF16)
+
+
+def run_experts(hidden, coefs, norm_gain, gate_weight, up_weight, down_weight):
+    peers, all_rows, cols = hidden.shape
+    units, width = gate_weight.shape
+    rows = all_rows // peers
+    shape = jax.ShapeDtypeStruct
+    return pl.pallas_call(
+        expert_kernel,
+        out_shape=(
+            shape((peers, rows, width), BF16),
+            shape((rows, width), F32),
+        ),
+        in_specs=[VMEM] * 5 + [ANY],
+        out_specs=(VMEM, VMEM),
+        scratch_shapes=[
+            pltpu.VMEM((SLOTS * CHUNK, width), BF16),
+            pltpu.VMEM((all_rows, width), F32),
+            pltpu.VMEM((all_rows, width), BF16),
+            pltpu.VMEM((all_rows, units), BF16),
+            pltpu.VMEM((all_rows, width), F32),
+            pltpu.SemaphoreType.DMA((SLOTS,)),
+        ],
+        compiler_params=pltpu.CompilerParams(vmem_limit_bytes=17 * 2**20),
+        name="experts",
+    )(
+        hidden,
+        coefs,
+        norm_gain[None],
+        pltpu.with_memory_space_constraint(gate_weight, pltpu.VMEM),
+        pltpu.with_memory_space_constraint(up_weight, pltpu.VMEM),
+        down_weight,
+    )
 
 
 def fused(
@@ -364,16 +427,7 @@
     shape = jax.ShapeDtypeStruct
     packet_width = channels + cols + LANES
 
-    new_state, packet = pl.pallas_call(
-        mixer_kernel,
-        out_shape=(
-            shape((rows,) + state_pool.shape[1:], BF16),
-            shape((peers, rows, packet_width), BF16),
-        ),
-        in_specs=[SMEM, SMEM] + [VMEM] * 13 + [SMEM],
-        out_specs=(VMEM, VMEM),
-        name="mixer",
-    )(
+    mixer_inputs = (
         slot_ids,
         expert_ids,
         conv_input,
@@ -389,8 +443,23 @@
         a_log,
         d_skip[None],
         residual,
-        expert_probs.astype(F32),
-    )
+        expert_probs,
+    )
+    new_state, packet = pl.pallas_call(
+        mixer_kernel,
+        out_shape=(
+            shape((rows,) + state_pool.shape[1:], BF16),
+            shape((peers, rows, packet_width), BF16),
+        ),
+        in_specs=[ANY] * len(mixer_inputs),
+        out_specs=(VMEM, VMEM),
+        scratch_shapes=[pltpu.SMEM(x.shape, x.dtype) for x in mixer_inputs[:2]]
+        + [pltpu.VMEM(x.shape, x.dtype) for x in mixer_inputs[2:]]
+        + [pltpu.SemaphoreType.DMA((len(mixer_inputs),))],
+        compiler_params=pltpu.CompilerParams(vmem_limit_bytes=6 * 2**20),
+        cost_estimate=beside(300000000),
+        name="mixer",
+    )(*(pltpu.with_memory_space_constraint(x, pltpu.HBM) for x in mixer_inputs))
     packets = lax.all_to_all(packet, "expert", split_axis=0, concat_axis=0, tiled=True)
     partial_mixed, residual_block, coefs = pl.pallas_call(
         project_kernel,
@@ -402,6 +471,8 @@
         in_specs=[VMEM] * 2,
         out_specs=(VMEM,) * 3,
         scratch_shapes=[pltpu.VMEM((all_rows, packet_width), F32)],
+        compiler_params=pltpu.CompilerParams(vmem_limit_bytes=6 * 2**20),
+        cost_estimate=beside(300000000),
         name="project",
     )(packets, out_weight)
     swap = [(i, halves - 1 - i) for i in range(halves)]
@@ -411,48 +482,32 @@
         out_shape=shape((peers, all_rows, cols), BF16),
         in_specs=[VMEM] * 3,
         out_specs=VMEM,
+        compiler_params=pltpu.CompilerParams(vmem_limit_bytes=2 * 2**20),
+        cost_estimate=beside(150000000),
         name="hidden",
     )(partial_mixed, other_mixed, residual_block)
     hidden = lax.all_to_all(hidden_copies, "expert", split_axis=0, concat_axis=0, tiled=True)
-    blocks = units // BLOCK
-    partial_out, own_rows = pl.pallas_call(
-        expert_kernel,
-        out_shape=(
-            shape((peers * halves, rows, width // halves), F32),
-            shape((rows, width), F32),
-        ),
-        in_specs=[VMEM] * 3 + [ANY] * 3,
-        out_specs=(VMEM, VMEM),
-        scratch_shapes=[
-            pltpu.VMEM((units, width), BF16),
-            pltpu.VMEM((units, width), BF16),
-            pltpu.VMEM((units, width), BF16),
-            pltpu.VMEM((all_rows, width), F32),
-            pltpu.VMEM((all_rows, width), BF16),
-            pltpu.VMEM((all_rows, units), BF16),
-            pltpu.VMEM((all_rows, width), F32),
-            pltpu.SemaphoreType.DMA((blocks,)),
-            pltpu.SemaphoreType.DMA((blocks,)),
-            pltpu.SemaphoreType.DMA((blocks,)),
-        ],
-        compiler_params=pltpu.CompilerParams(vmem_limit_bytes=60 * 2**20),
-        name="experts",
-    )(hidden, coefs, norm_gain[None], gate_weight, up_weight, down_weight)
-    pieces = lax.all_to_all(
-        partial_out, ("expert", "tensor"), split_axis=0, concat_axis=0, tiled=True
-    )
-    half_out = pl.pallas_call(
+    partial_out, own_rows = run_experts(
+        hidden, coefs, norm_gain, gate_weight, up_weight, down_weight
+    )
+    pieces = lax.all_to_all(partial_out, "expert", split_axis=0, concat_axis=0, tiled=True)
+    routed = pl.pallas_call(
         sum_kernel,
-        out_shape=shape((rows, width // halves), BF16),
-        in_specs=[VMEM] * 2,
+        out_shape=shape((rows, width), F32),
+        in_specs=[VMEM],
         out_specs=VMEM,
+        compiler_params=pltpu.CompilerParams(vmem_limit_bytes=2 * 2**20),
         name="sum",
-    )(pieces, own_rows)
-    other_half = lax.ppermute(half_out, "tensor", swap)
-    first = lax.axis_index("tensor") == 0
-    layer_out = jnp.concatenate(
-        [jnp.where(first, half_out, other_half), jnp.where(first, other_half, half_out)], axis=1
-    )
+    )(pieces)
+    other_routed = lax.ppermute(routed, "tensor", swap)
+    layer_out = pl.pallas_call(
+        output_kernel,
+        out_shape=shape((rows, width), BF16),
+        in_specs=[VMEM] * 3,
+        out_specs=VMEM,
+        compiler_params=pltpu.CompilerParams(vmem_limit_bytes=2 * 2**20),
+        name="output",
+    )(routed, other_routed, own_rows)
     return (layer_out, new_state)
 
 

time: 80.5 us -> 56.1 us (0.70)
  Pallas kernels: 32.6 us -> 17.6 us
  blocking collectives: 40.6 us -> 34.9 us
  other arithmetic: 2.56 us -> 0.01 us
    pallas_call x2 -> x3, Pallas kernels: 25 us -> 14.1 us  [the longest x1 13.5 us: run_experts(): pl.pallas_call(expert_kernel, out_shape=(shape((peers, rows, width), BF16...]
    all_to_all x1, blocking collectives: 14.2 us -> 9.84 us  [fused(): lax.all_to_all(partial_out, 'expert', split_axis=0, concat_axis=0, tiled=...]
    pallas_call x1, Pallas kernels: 3.55 us -> 0.66 us  [fused(): pl.pallas_call(project_kernel, out_shape=(shape((all_rows, cols), F32), s...]
    pallas_call x1, Pallas kernels: 1.45 us -> 0.02 us  [fused(): pl.pallas_call(hidden_kernel, out_shape=shape((peers, all_rows, cols), BF...]
    convert_element_type x1 -> x0, other arithmetic: 1.22 us -> none  [fused(): expert_probs.astype(F32)]
    all_to_all x1, blocking collectives: 11.6 us -> 10.5 us  [fused(): lax.all_to_all(hidden_copies, 'expert', split_axis=0, concat_axis=0, tile...]
where the time goes in v2:
time: 56.1 us; the launch traced here: 55.9 us
  blocking collectives  34.9 us (62%)
  Pallas kernels  17.6 us (31%)
  waiting for transfers between devices  2.41 us (4%)
  between operations  0.81 us (1%)
    all_to_all x1, blocking collectives, fused(): lax.all_to_all(packet, 'expert', split_axis=0, concat_axis=0, tiled=True)  14.5 us
    pallas_call x1, Pallas kernels, run_experts(): pl.pallas_call(expert_kernel, out_shape=(shape((peers, rows, width), BF16...  13.5 us
    all_to_all x1, blocking collectives, fused(): lax.all_to_all(hidden_copies, 'expert', split_axis=0, concat_axis=0, tile...  10.5 us
    all_to_all x1, blocking collectives, fused(): lax.all_to_all(partial_out, 'expert', split_axis=0, concat_axis=0, tiled=...  9.84 us
    pallas_call x1, Pallas kernels, fused(): pl.pallas_call(mixer_kernel, out_shape=(shape((rows,) + state_pool.shape[...  2.8 us
    ppermute x1, waiting for transfers between devices, fused(): other_mixed = lax.ppermute(partial_mixed, 'tensor', swap)  1.22 us
    ppermute x1, waiting for transfers between devices, fused(): other_routed = lax.ppermute(routed, 'tensor', swap)  1.19 us
  transfers between devices with their start and end apart: 2, of which 2 were waited for; matrix products, arithmetic and copies ran while one was open for 0% of the time, Pallas kernels for 0%

profile of v2, /device:TPU:0, one launch (start us, length us, event | category | flops | bytes accessed | tf_op | source)
XLA Modules:
  0.0 55.9 jit_solution(6498424193803798782)
XLA Ops:
  0.6 0.0 copy-start.1
  0.6 2.8 %mixer.1 = (bf16[2,16,4096]{2,1,0:T(8,128)(2,1)}, bf16[8,2,4736]{2,1,0:T(2,128)(2,1)S(1)}) custom-call(s32[2]{0:T(128)} %refs_0_.1, s32[2,2]{1,0:T(2,128)} %refs_1_.1, bf16[2,4096]{1,0:T(2,128)(2,1)} %refs_2_.1, bf16[2,4096]{1,0:T(2,128)(2,1)} %refs_3_.1, bf16[2,4096]{1,0:T(2,128)(2,1)} %refs_4_.1, f32[2,16]{1,0:T(2,128)} %refs_5_.1, f32[2,16]{1,0:T(2,128)} %refs_6_.1, ...), custom_call_target="tpu_custom_call" | custom-call | flops 89999998976 | bytes 300000000 | tf_op jit(solution)/shard_map/mixer/pallas_call | solution.py:448
  3.5 14.5 %all_to_all.15.packets = bf16[8,2,4736]{2,1,0:T(2,128)(2,1)S(1)} all-to-all(bf16[8,2,4736]{2,1,0:T(2,128)(2,1)S(1)} %get-tuple-element.9), channel_id=1, replica_groups=mesh['groups'=2,'expert'=8,'tensor'=2] {'expert'}, dimensions={0} | all-to-all | bytes 303104 | tf_op jit(solution)/shard_map/all_to_all | solution.py:463
  18.0 0.0 copy-done.1
  18.0 0.0 slice-start
  18.0 0.0 slice-start.1
  18.0 0.0 slice-start.2
  18.0 0.0 slice-start.3
  18.0 0.0 slice-start.5
  18.0 0.0 slice-start.6
  18.0 0.0 slice-start.7
  18.0 0.0 slice-start.8
  18.1 0.7 %project.1 = (f32[16,512]{1,0:T(8,128)S(1)}, f32[16,512]{1,0:T(8,128)S(1)}, f32[16,128]{1,0:T(8,128)S(1)}) custom-call(bf16[8,2,4736]{2,1,0:T(2,128)(2,1)S(1)} %all_to_all.15.packets, bf16[4096,512]{1,0:T(8,128)(2,1)S(1)} %copy-done.1), custom_call_target="tpu_custom_call" | custom-call | flops 89999998976 | bytes 300000000 | tf_op jit(solution)/shard_map/project/pallas_call | solution.py:464
  18.7 0.0 collective-permute-start
  18.7 1.2 %collective-permute-done.other = f32[16,512]{1,0:T(8,128)S(1)} collective-permute-done((f32[16,512]{1,0:T(8,128)S(1)}, f32[16,512]{1,0:T(8,128)S(1)}, u32[]{:S(2)}, u32[]{:S(2)}) %collective-permute-start) | collective-permute-done | bytes 32800 | tf_op jit(solution)/shard_map/ppermute | solution.py:479
  20.0 10.5 %all_to_all.16.hidden = bf16[8,16,512]{2,1,0:T(8,128)(2,1)S(1)} all-to-all(bf16[8,16,512]{2,1,0:T(8,128)(2,1)S(1)} %hidden.1), channel_id=1, replica_groups=mesh['groups'=2,'expert'=8,'tensor'=2] {'expert'}, dimensions={0} | all-to-all | bytes 262144 | tf_op jit(solution)/shard_map/all_to_all | solution.py:489
  30.5 0.0 slice-done
  30.5 0.0 slice-done.1
  30.5 0.0 slice-done.2
  30.5 0.0 slice-done.3
  30.5 0.0 slice-done.5
  30.5 0.0 slice-done.6
  30.5 0.0 slice-done.7
  30.5 0.0 slice-done.8
  30.5 0.0 slice-done.4
  30.5 0.0 slice-done.9
  30.6 0.0 copy-done
  30.6 13.5 %experts.1 = (bf16[8,2,4096]{2,1,0:T(2,128)(2,1)S(1)}, f32[2,4096]{1,0:T(2,128)S(1)}) custom-call(bf16[8,16,512]{2,1,0:T(8,128)(2,1)S(1)} %all_to_all.16.hidden, f32[16,128]{1,0:T(8,128)S(1)} %get-tuple-element.12.coefs, f32[1,4096]{1,0:T(1,128)S(1)} %bitcast.9, bf16[2304,4096]{1,0:T(8,128)(2,1)S(1)} %bitcast.6, bf16[2304,4096]{1,0:T(8,128)(2,1)S(1)} %bitcast.8, ...), custom_call_target="tpu_custom_call" | custom-call | tf_op jit(solution)/shard_map/experts/pallas_call | solution.py:369
  44.1 9.8 %all_to_all.17.pieces = bf16[8,2,4096]{2,1,0:T(2,128)(2,1)S(1)} all-to-all(bf16[8,2,4096]{2,1,0:T(2,128)(2,1)S(1)} %get-tuple-element.13), channel_id=1, replica_groups=mesh['groups'=2,'expert'=8,'tensor'=2] {'expert'}, dimensions={0} | all-to-all | bytes 262144 | tf_op jit(solution)/shard_map/all_to_all | solution.py:493
  54.0 0.1 collective-permute-start.1
  54.0 1.2 %collective-permute-done.1.other = f32[2,4096]{1,0:T(2,128)S(1)} collective-permute-done((f32[2,4096]{1,0:T(2,128)S(1)}, f32[2,4096]{1,0:T(2,128)S(1)}, u32[]{:S(2)}, u32[]{:S(2)}) %collective-permute-start.1) | collective-permute-done | bytes 32800 | tf_op jit(solution)/shard_map/ppermute | solution.py:502
  55.2 0.6 %output.1 = bf16[2,4096]{1,0:T(2,128)(2,1)} custom-call(f32[2,4096]{1,0:T(2,128)S(1)} %sum.1.mine, f32[2,4096]{1,0:T(2,128)S(1)} %collective-permute-done.1.other, f32[2,4096]{1,0:T(2,128)S(1)} %get-tuple-element.14.own_rows), custom_call_target="tpu_custom_call" | custom-call | tf_op jit(solution)/shard_map/output/pallas_call | solution.py:503
  (7 shorter events, 0.0 us)
Async XLA Ops:
  0.6 17.4 %copy-start.1 = (bf16[4096,512]{1,0:T(8,128)(2,1)S(1)}, bf16[4096,512]{1,0:T(8,128)(2,1)}, u32[]{:S(2)}) copy-start(bf16[4096,512]{1,0:T(8,128)(2,1)} %out_weight.1) | copy-start | bytes 12582916
  18.0 12.5 %slice-start = ((s8[18874368]{0:T(1024)(128)(4,1)}), s8[4194304]{0:T(1024)(128)(4,1)S(1)}, s32[]{:S(2)}) async-start(s8[18874368]{0:T(1024)(128)(4,1)} %bitcast.5), calls=%async_computation.3 | async-start | bytes 8388608
  18.0 12.5 %slice-start.1 = ((s8[18874368]{0:T(1024)(128)(4,1)}), s8[4194304]{0:T(1024)(128)(4,1)S(1)}, s32[]{:S(2)}) async-start(s8[18874368]{0:T(1024)(128)(4,1)} %bitcast.5), calls=%async_computation.4 | async-start | bytes 8388608
  18.0 12.5 %slice-start.2 = ((s8[18874368]{0:T(1024)(128)(4,1)}), s8[4194304]{0:T(1024)(128)(4,1)S(1)}, s32[]{:S(2)}) async-start(s8[18874368]{0:T(1024)(128)(4,1)} %bitcast.5), calls=%async_computation.5 | async-start | bytes 8388608
  18.0 12.5 %slice-start.3 = ((s8[18874368]{0:T(1024)(128)(4,1)}), s8[4194304]{0:T(1024)(128)(4,1)S(1)}, s32[]{:S(2)}) async-start(s8[18874368]{0:T(1024)(128)(4,1)} %bitcast.5), calls=%async_computation.6 | async-start | bytes 8388608
  18.0 12.5 %slice-start.5 = ((s8[18874368]{0:T(1024)(128)(4,1)}), s8[4194304]{0:T(1024)(128)(4,1)S(1)}, s32[]{:S(2)}) async-start(s8[18874368]{0:T(1024)(128)(4,1)} %bitcast.7), calls=%async_computation.8 | async-start | bytes 8388608
  18.0 12.5 %slice-start.6 = ((s8[18874368]{0:T(1024)(128)(4,1)}), s8[4194304]{0:T(1024)(128)(4,1)S(1)}, s32[]{:S(2)}) async-start(s8[18874368]{0:T(1024)(128)(4,1)} %bitcast.7), calls=%async_computation.9 | async-start | bytes 8388608
  18.0 12.5 %slice-start.7 = ((s8[18874368]{0:T(1024)(128)(4,1)}), s8[4194304]{0:T(1024)(128)(4,1)S(1)}, s32[]{:S(2)}) async-start(s8[18874368]{0:T(1024)(128)(4,1)} %bitcast.7), calls=%async_computation.10 | async-start | bytes 8388608
  18.0 12.5 %slice-start.8 = ((s8[18874368]{0:T(1024)(128)(4,1)}), s8[4194304]{0:T(1024)(128)(4,1)S(1)}, s32[]{:S(2)}) async-start(s8[18874368]{0:T(1024)(128)(4,1)} %bitcast.7), calls=%async_computation.11 | async-start | bytes 8388608
  18.7 1.2 %collective-permute-start = (f32[16,512]{1,0:T(8,128)S(1)}, f32[16,512]{1,0:T(8,128)S(1)}, u32[]{:S(2)}, u32[]{:S(2)}) collective-permute-start(f32[16,512]{1,0:T(8,128)S(1)} %get-tuple-element.10.mine), channel_id=1, source_target_pairs={{0,1},{1,0},{2,3},{3,2},{4,5},{5,4},{6,7},{7,6},{8,9},{9,8},{10,11... | collective-permute-start | bytes 98312 | tf_op jit(solution)/shard_map/ppermute | solution.py:479
  19.9 10.6 %slice-start.4 = ((s8[18874368]{0:T(1024)(128)(4,1)}), s8[2097152]{0:T(1024)(128)(4,1)S(1)}, s32[]{:S(2)}) async-start(s8[18874368]{0:T(1024)(128)(4,1)} %bitcast.5), calls=%async_computation.7 | async-start | bytes 4194304
  19.9 10.6 %slice-start.9 = ((s8[18874368]{0:T(1024)(128)(4,1)}), s8[2097152]{0:T(1024)(128)(4,1)S(1)}, s32[]{:S(2)}) async-start(s8[18874368]{0:T(1024)(128)(4,1)} %bitcast.7), calls=%async_computation.12 | async-start | bytes 4194304
  19.9 10.6 %copy-start = (f32[4096]{0:T(1024)S(1)}, f32[4096]{0:T(1024)}, u32[]{:S(2)}) copy-start(f32[4096]{0:T(1024)} %param.36) | copy-start | bytes 49156
  54.0 1.3 %collective-permute-start.1 = (f32[2,4096]{1,0:T(2,128)S(1)}, f32[2,4096]{1,0:T(2,128)S(1)}, u32[]{:S(2)}, u32[]{:S(2)}) collective-permute-start(f32[2,4096]{1,0:T(2,128)S(1)} %sum.1.mine), channel_id=1, source_target_pairs={{0,1},{1,0},{2,3},{3,2},{4,5},{5,4},{6,7},{7,6},{8,9},{9,8},{10,11... | collective-permute-start | bytes 98312 | tf_op jit(solution)/shard_map/ppermute | solution.py:502

commit v3 on v2

--- a/solution.py
+++ b/solution.py
@@ -148,8 +148,7 @@
 
 
 LANES = 128
-BLOCK = 768
-CHUNK = 384
+BLOCK = 256
 SLOTS = 5
 EPS = 1e-05
 VMEM = pl.BlockSpec(memory_space=pltpu.VMEM)
@@ -183,8 +182,10 @@
     ]
     for copy in copies:
         copy.start()
-    for copy in copies:
-        copy.wait()
+    late = (7, 12)
+    for i, copy in enumerate(copies):
+        if i not in late:
+            copy.wait()
     (
         slot_ref,
         ids_ref,
@@ -207,7 +208,6 @@
     peers = packet.shape[0]
     cols = residual.shape[1] // peers
     first_slot = lax.axis_index("expert") * state_pool.shape[0]
-    rates = -jnp.exp(a_log[...])
     lane = lax.broadcasted_iota(jnp.int32, (1, LANES), 1)
     row = lax.broadcasted_iota(jnp.int32, (rows, channels), 0)
     slots = [slot_ref[r] - first_slot for r in range(rows)]
@@ -226,6 +226,9 @@
     gates = gate_input[...].astype(F32)
     gates = gates * jax.nn.sigmoid(gates)
     skips = d_skip[...] * conv_outs
+    for i in late:
+        copies[i].wait()
+    rates = -jnp.exp(a_log[...])
     for r in range(rows):
         b = lane_to_sublane(b_proj[r : r + 1, :])
         c = lane_to_sublane(c_proj[r : r + 1, :])
@@ -275,31 +278,38 @@
     down_hbm,
     partial,
     own_rows,
+    turned,
     down_buf,
     wide,
     normed,
     units_out,
-    total,
     down_sem,
 ):
     units, width = gate_weight.shape
     peers, rows, cols = hidden.shape
     blocks = units // BLOCK
 
-    chunks = units // CHUNK
-    slots = down_buf.shape[0] // CHUNK
-
-    def down_copy(i):
-        slot = i % slots
-        return pltpu.make_async_copy(
-            down_hbm.at[pl.ds(i * CHUNK, CHUNK)],
-            down_buf.at[pl.ds(slot * CHUNK, CHUNK)],
-            down_sem.at[slot],
-        )
-
-    for i in range(slots):
+    steps = units // BLOCK
+    slots = down_buf.shape[0]
+
+    def down_copy(step):
+        slot = lax.rem(step, slots)
+        rows = pl.ds(step * BLOCK, BLOCK)
+        return pltpu.make_async_copy(down_hbm.at[rows], down_buf.at[slot], down_sem.at[slot])
+
+    def start_copy(i, carry):
         down_copy(i).start()
-
+        return carry
+
+    lax.fori_loop(0, slots, start_copy, 0)
+    half = BLOCK // 2
+
+    def turn(step):
+        part = pl.ds(step * BLOCK + half, half)
+        turned[step % 2, :, 0:half] = gate_weight[part, :].T
+        turned[step % 2, :, half:] = up_weight[part, :].T
+
+    turn(0)
     for d in range(peers):
         wide[:, d * cols : (d + 1) * cols] = hidden[d].astype(F32)
     mean = jnp.sum(wide[...] * wide[...], axis=1, keepdims=True) * (1.0 / width)
@@ -319,32 +329,46 @@
     upper_coef = jnp.sum(jnp.where(lane == lower + 1, coefs[...], 0.0), axis=1, keepdims=True)
     dims = (((1,), (1,)), ((), ()))
 
-    def unit_block(i, carry):
-        start = pl.multiple_of(i * BLOCK, BLOCK)
-        part = pl.ds(start, BLOCK)
+    def finish(start, gate, up):
+        column = lax.broadcasted_iota(jnp.int32, gate.shape, 1) + start
+        coef = jnp.where(column < boundary, lower_coef, upper_coef)
+        hidden_units = gate * jax.nn.sigmoid(gate) * up * coef
+        units_out[:, start : start + gate.shape[1]] = hidden_units.astype(BF16)
+
+    total = wide
+
+    def unit_step(step):
+        start = step * BLOCK
+        if step + 1 < steps:
+            turn(step + 1)
+        part = pl.ds(start, half)
         gate = lax.dot_general(normed[...], gate_weight[part, :], dims, preferred_element_type=F32)
         up = lax.dot_general(normed[...], up_weight[part, :], dims, preferred_element_type=F32)
-        column = lax.broadcasted_iota(jnp.int32, (rows, BLOCK), 1) + start
-        coef = jnp.where(column < boundary, lower_coef, upper_coef)
-        units_out[:, part] = (gate * jax.nn.sigmoid(gate) * up * coef).astype(BF16)
-        return carry
-
-    lax.fori_loop(0, blocks, unit_block, 0)
-    first = 0
-    while first < chunks:
-        slot = first % slots
-        count = min(BLOCK // CHUNK, chunks - first, slots - slot)
-        for i in range(first, first + count):
-            down_copy(i).wait()
+        finish(start, gate, up)
+        both = jnp.dot(normed[...], turned[step % 2], preferred_element_type=F32)
+        finish(start + half, both[:, 0:half], both[:, half:])
+
+    def down_step(step):
         product = jnp.dot(
-            units_out[:, first * CHUNK : (first + count) * CHUNK],
-            down_buf[slot * CHUNK : (slot + count) * CHUNK, :],
+            units_out[:, step * BLOCK : (step + 1) * BLOCK],
+            down_buf[step % slots],
             preferred_element_type=F32,
         )
-        total[...] = product if first == 0 else total[...] + product
-        for i in range(first + slots, min(first + count + slots, chunks)):
-            down_copy(i).start()
-        first += count
+        total[...] = product if step == 0 else total[...] + product
+
+    for step in range(steps + 1):
+        if step > 0:
+            down_copy(step - 1).wait()
+
+        @pl.when(lower >= 0)
+        def _():
+            if step > 0:
+                down_step(step - 1)
+            if step < steps:
+                unit_step(step)
+
+        if step > 0 and step - 1 + slots < steps:
+            down_copy(step - 1 + slots).start()
 
     for d in range(peers):
         partial[d] = total[d * own : (d + 1) * own, :].astype(BF16)
@@ -375,14 +399,14 @@
         in_specs=[VMEM] * 5 + [ANY],
         out_specs=(VMEM, VMEM),
         scratch_shapes=[
-            pltpu.VMEM((SLOTS * CHUNK, width), BF16),
+            pltpu.VMEM((2, width, BLOCK), BF16),
+            pltpu.VMEM((SLOTS, BLOCK, width), BF16),
             pltpu.VMEM((all_rows, width), F32),
             pltpu.VMEM((all_rows, width), BF16),
             pltpu.VMEM((all_rows, units), BF16),
-            pltpu.VMEM((all_rows, width), F32),
             pltpu.SemaphoreType.DMA((SLOTS,)),
         ],
-        compiler_params=pltpu.CompilerParams(vmem_limit_bytes=17 * 2**20),
+        compiler_params=pltpu.CompilerParams(vmem_limit_bytes=16 * 2**20),
         name="experts",
     )(
         hidden,
@@ -392,6 +416,45 @@
         pltpu.with_memory_space_constraint(up_weight, pltpu.VMEM),
         down_weight,
     )
+
+
+def run_mixer(peers, cols, conv_input, gate_input, step_input, b_proj, c_proj, slot_ids, state_pool, conv_pool, conv_weight, conv_bias, step_bias, a_log, d_skip, residual, expert_ids, expert_probs):
+    rows, channels = conv_input.shape
+    packet_width = channels + cols + LANES
+    shape = jax.ShapeDtypeStruct
+    mixer_inputs = (
+        slot_ids,
+        expert_ids,
+        conv_input,
+        gate_input,
+        step_input,
+        b_proj,
+        c_proj,
+        state_pool,
+        jnp.transpose(conv_pool, (1, 0, 2)),
+        conv_weight,
+        conv_bias[None],
+        step_bias[None],
+        a_log,
+        d_skip[None],
+        residual,
+        expert_probs,
+    )
+    return pl.pallas_call(
+        mixer_kernel,
+        out_shape=(
+            pltpu.VMEM((rows,) + state_pool.shape[1:], BF16),
+            shape((peers, rows, packet_width), BF16),
+        ),
+        in_specs=[ANY] * len(mixer_inputs),
+        out_specs=(VMEM, VMEM),
+        scratch_shapes=[pltpu.SMEM(x.shape, x.dtype) for x in mixer_inputs[:2]]
+        + [pltpu.VMEM(x.shape, x.dtype) for x in mixer_inputs[2:]]
+        + [pltpu.SemaphoreType.DMA((len(mixer_inputs),))],
+        compiler_params=pltpu.CompilerParams(vmem_limit_bytes=6 * 2**20),
+        cost_estimate=beside(300000000),
+        name="mixer",
+    )(*(pltpu.with_memory_space_constraint(x, pltpu.HBM) for x in mixer_inputs))
 
 
 def fused(
@@ -427,39 +490,26 @@
     shape = jax.ShapeDtypeStruct
     packet_width = channels + cols + LANES
 
-    mixer_inputs = (
-        slot_ids,
-        expert_ids,
+    new_state, packet = run_mixer(
+        peers,
+        cols,
         conv_input,
         gate_input,
         step_input,
         b_proj,
         c_proj,
+        slot_ids,
         state_pool,
-        jnp.transpose(conv_pool, (1, 0, 2)),
+        conv_pool,
         conv_weight,
-        conv_bias[None],
-        step_bias[None],
+        conv_bias,
+        step_bias,
         a_log,
-        d_skip[None],
+        d_skip,
         residual,
+        expert_ids,
         expert_probs,
     )
-    new_state, packet = pl.pallas_call(
-        mixer_kernel,
-        out_shape=(
-            shape((rows,) + state_pool.shape[1:], BF16),
-            shape((peers, rows, packet_width), BF16),
-        ),
-        in_specs=[ANY] * len(mixer_inputs),
-        out_specs=(VMEM, VMEM),
-        scratch_shapes=[pltpu.SMEM(x.shape, x.dtype) for x in mixer_inputs[:2]]
-        + [pltpu.VMEM(x.shape, x.dtype) for x in mixer_inputs[2:]]
-        + [pltpu.SemaphoreType.DMA((len(mixer_inputs),))],
-        compiler_params=pltpu.CompilerParams(vmem_limit_bytes=6 * 2**20),
-        cost_estimate=beside(300000000),
-        name="mixer",
-    )(*(pltpu.with_memory_space_constraint(x, pltpu.HBM) for x in mixer_inputs))
     packets = lax.all_to_all(packet, "expert", split_axis=0, concat_axis=0, tiled=True)
     partial_mixed, residual_block, coefs = pl.pallas_call(
         project_kernel,
@@ -516,6 +566,7 @@
     tiled = (
         out_weight.shape[1] % LANES == 0
         and gate_weight.shape[0] % BLOCK == 0
+        and gate_weight.shape[0] // BLOCK >= SLOTS
         and lax.axis_size("tensor") == 2
     )
     return fused(*args) if tiled else local(*args)

time: 56.1 us -> 54.2 us (0.966)
  Pallas kernels: 17.6 us -> 15.7 us
  local copies, waits for them, and re-layouts: 0.05 us -> 0.76 us
  waiting for transfers between devices: 2.41 us -> 1.71 us
    pallas_call x1, Pallas kernels: 13.5 us -> 12.4 us  [run_experts(): pl.pallas_call(expert_kernel, out_shape=(shape((peers, rows, width), BF16...]
    pallas_call x1, Pallas kernels: 2.8 us -> 2 us  [run_mixer(): pl.pallas_call(mixer_kernel, out_shape=(pltpu.VMEM((rows,) + state_pool.s...]
    ppermute x1, waiting for transfers between devices: 1.19 us -> 0.49 us  [fused(): other_routed = lax.ppermute(routed, 'tensor', swap)]
    unnamed x24 -> x25, local copies, waits for them, and re-layouts: 0.05 us -> 0.76 us
  transfers between devices with their start and end apart: 2 -> 2, of which waited for: 2 -> 2; matrix products, arithmetic and copies ran while one was open for 0% -> 1% of each run, Pallas kernels for 0% -> 0%
where the time goes in v3:
time: 54.2 us; the launch traced here: 53.9 us
  blocking collectives  34.9 us (64%)
  Pallas kernels  15.7 us (29%)
  waiting for transfers between devices  1.71 us (3%)
  between operations  0.81 us (1%)
  local copies, waits for them, and re-layouts  0.76 us (1%)
    all_to_all x1, blocking collectives, fused(): lax.all_to_all(packet, 'expert', split_axis=0, concat_axis=0, tiled=True)  14.5 us
    pallas_call x1, Pallas kernels, run_experts(): pl.pallas_call(expert_kernel, out_shape=(shape((peers, rows, width), BF16...  12.4 us
    all_to_all x1, blocking collectives, fused(): lax.all_to_all(hidden_copies, 'expert', split_axis=0, concat_axis=0, tile...  10.5 us
    all_to_all x1, blocking collectives, fused(): lax.all_to_all(partial_out, 'expert', split_axis=0, concat_axis=0, tiled=...  9.84 us
    pallas_call x1, Pallas kernels, run_mixer(): pl.pallas_call(mixer_kernel, out_shape=(pltpu.VMEM((rows,) + state_pool.s...  2 us
    ppermute x1, waiting for transfers between devices, fused(): other_mixed = lax.ppermute(partial_mixed, 'tensor', swap)  1.22 us
  transfers between devices with their start and end apart: 2, of which 2 were waited for; matrix products, arithmetic and copies ran while one was open for 1% of the time, Pallas kernels for 0%

profile of v3, /device:TPU:0, one launch (start us, length us, event | category | flops | bytes accessed | tf_op | source)
XLA Modules:
  0.0 53.9 jit_solution(1272856550566503194)
XLA Ops:
  0.6 0.0 copy-start.1
  0.6 2.0 %mixer.1 = (bf16[2,16,4096]{2,1,0:T(8,128)(2,1)S(1)}, bf16[8,2,4736]{2,1,0:T(2,128)(2,1)S(1)}) custom-call(s32[2]{0:T(128)} %refs_0_.1, s32[2,2]{1,0:T(2,128)} %refs_1_.1, bf16[2,4096]{1,0:T(2,128)(2,1)} %refs_2_.1, bf16[2,4096]{1,0:T(2,128)(2,1)} %refs_3_.1, bf16[2,4096]{1,0:T(2,128)(2,1)} %refs_4_.1, f32[2,16]{1,0:T(2,128)} %refs_5_.1, f32[2,16]{1,0:T(2,128)} %refs_6_.1, ...), custom_call_target="tpu_custom_call" | custom-call | flops 89999998976 | bytes 300000000 | tf_op jit(solution)/shard_map/mixer/pallas_call | solution.py:443
  2.7 14.5 %all_to_all.15.packets = bf16[8,2,4736]{2,1,0:T(2,128)(2,1)S(1)} all-to-all(bf16[8,2,4736]{2,1,0:T(2,128)(2,1)S(1)} %get-tuple-element.9), channel_id=1, replica_groups=mesh['groups'=2,'expert'=8,'tensor'=2] {'expert'}, dimensions={0} | all-to-all | bytes 303104 | tf_op jit(solution)/shard_map/all_to_all | solution.py:513
  17.2 0.0 copy-done.1
  17.2 0.0 slice-start
  17.2 0.0 slice-start.1
  17.2 0.0 slice-start.3
  17.2 0.0 slice-start.5
  17.2 0.0 slice-start.6
  17.2 0.0 slice-start.7
  17.3 0.0 slice-start.8
  17.3 0.7 %project.1 = (f32[16,512]{1,0:T(8,128)S(1)}, f32[16,512]{1,0:T(8,128)S(1)}, f32[16,128]{1,0:T(8,128)S(1)}) custom-call(bf16[8,2,4736]{2,1,0:T(2,128)(2,1)S(1)} %all_to_all.15.packets, bf16[4096,512]{1,0:T(8,128)(2,1)S(1)} %copy-done.1), custom_call_target="tpu_custom_call" | custom-call | flops 89999998976 | bytes 300000000 | tf_op jit(solution)/shard_map/project/pallas_call | solution.py:514
  17.9 0.0 collective-permute-start
  17.9 1.2 %collective-permute-done.other = f32[16,512]{1,0:T(8,128)S(1)} collective-permute-done((f32[16,512]{1,0:T(8,128)S(1)}, f32[16,512]{1,0:T(8,128)S(1)}, u32[]{:S(2)}, u32[]{:S(2)}) %collective-permute-start) | collective-permute-done | bytes 32800 | tf_op jit(solution)/shard_map/ppermute | solution.py:529
  19.2 10.5 %all_to_all.16.hidden = bf16[8,16,512]{2,1,0:T(8,128)(2,1)S(1)} all-to-all(bf16[8,16,512]{2,1,0:T(8,128)(2,1)S(1)} %hidden.1), channel_id=1, replica_groups=mesh['groups'=2,'expert'=8,'tensor'=2] {'expert'}, dimensions={0} | all-to-all | bytes 262144 | tf_op jit(solution)/shard_map/all_to_all | solution.py:539
  29.7 0.0 slice-done
  29.7 0.0 slice-done.1
  29.7 0.0 slice-done.2
  29.7 0.0 slice-done.3
  29.7 0.0 slice-done.5
  29.7 0.0 slice-done.6
  29.7 0.0 slice-done.7
  29.7 0.0 slice-done.8
  29.7 0.0 slice-done.4
  29.7 0.0 slice-done.9
  29.8 0.0 copy-done
  29.8 12.4 %experts.1 = (bf16[8,2,4096]{2,1,0:T(2,128)(2,1)S(1)}, f32[2,4096]{1,0:T(2,128)S(1)}) custom-call(bf16[8,16,512]{2,1,0:T(8,128)(2,1)S(1)} %all_to_all.16.hidden, f32[16,128]{1,0:T(8,128)S(1)} %get-tuple-element.12.coefs, f32[1,4096]{1,0:T(1,128)S(1)} %bitcast.9, bf16[2304,4096]{1,0:T(8,128)(2,1)S(1)} %bitcast.6, bf16[2304,4096]{1,0:T(8,128)(2,1)S(1)} %bitcast.8, ...), custom_call_target="tpu_custom_call" | custom-call | tf_op jit(solution)/shard_map/experts/pallas_call | solution.py:393
  42.2 9.8 %all_to_all.17.pieces = bf16[8,2,4096]{2,1,0:T(2,128)(2,1)S(1)} all-to-all(bf16[8,2,4096]{2,1,0:T(2,128)(2,1)S(1)} %get-tuple-element.13), channel_id=1, replica_groups=mesh['groups'=2,'expert'=8,'tensor'=2] {'expert'}, dimensions={0} | all-to-all | bytes 262144 | tf_op jit(solution)/shard_map/all_to_all | solution.py:543
  52.0 0.1 collective-permute-start.1
  52.1 0.7 %copy.23 = bf16[2,16,4096]{2,1,0:T(8,128)(2,1)} copy(bf16[2,16,4096]{2,1,0:T(8,128)(2,1)S(1)} %get-tuple-element.17) | data formatting | bytes 524288
  52.8 0.5 collective-permute-done.1.other
  53.3 0.6 %output.1 = bf16[2,4096]{1,0:T(2,128)(2,1)} custom-call(f32[2,4096]{1,0:T(2,128)S(1)} %sum.1.mine, f32[2,4096]{1,0:T(2,128)S(1)} %collective-permute-done.1.other, f32[2,4096]{1,0:T(2,128)S(1)} %get-tuple-element.14.own_rows), custom_call_target="tpu_custom_call" | custom-call | tf_op jit(solution)/shard_map/output/pallas_call | solution.py:553
  (8 shorter events, 0.0 us)
Async XLA Ops:
  0.6 16.6 %copy-start.1 = (bf16[4096,512]{1,0:T(8,128)(2,1)S(1)}, bf16[4096,512]{1,0:T(8,128)(2,1)}, u32[]{:S(2)}) copy-start(bf16[4096,512]{1,0:T(8,128)(2,1)} %out_weight.1) | copy-start | bytes 12582916
  17.2 12.5 %slice-start = ((s8[18874368]{0:T(1024)(128)(4,1)}), s8[4194304]{0:T(1024)(128)(4,1)S(1)}, s32[]{:S(2)}) async-start(s8[18874368]{0:T(1024)(128)(4,1)} %bitcast.5), calls=%async_computation.3 | async-start | bytes 8388608
  17.2 12.5 %slice-start.1 = ((s8[18874368]{0:T(1024)(128)(4,1)}), s8[4194304]{0:T(1024)(128)(4,1)S(1)}, s32[]{:S(2)}) async-start(s8[18874368]{0:T(1024)(128)(4,1)} %bitcast.5), calls=%async_computation.4 | async-start | bytes 8388608
  17.2 12.5 %slice-start.2 = ((s8[18874368]{0:T(1024)(128)(4,1)}), s8[4194304]{0:T(1024)(128)(4,1)S(1)}, s32[]{:S(2)}) async-start(s8[18874368]{0:T(1024)(128)(4,1)} %bitcast.5), calls=%async_computation.5 | async-start | bytes 8388608
  17.2 12.5 %slice-start.3 = ((s8[18874368]{0:T(1024)(128)(4,1)}), s8[4194304]{0:T(1024)(128)(4,1)S(1)}, s32[]{:S(2)}) async-start(s8[18874368]{0:T(1024)(128)(4,1)} %bitcast.5), calls=%async_computation.6 | async-start | bytes 8388608
  17.2 12.5 %slice-start.5 = ((s8[18874368]{0:T(1024)(128)(4,1)}), s8[4194304]{0:T(1024)(128)(4,1)S(1)}, s32[]{:S(2)}) async-start(s8[18874368]{0:T(1024)(128)(4,1)} %bitcast.7), calls=%async_computation.8 | async-start | bytes 8388608
  17.2 12.5 %slice-start.6 = ((s8[18874368]{0:T(1024)(128)(4,1)}), s8[4194304]{0:T(1024)(128)(4,1)S(1)}, s32[]{:S(2)}) async-start(s8[18874368]{0:T(1024)(128)(4,1)} %bitcast.7), calls=%async_computation.9 | async-start | bytes 8388608
  17.2 12.5 %slice-start.7 = ((s8[18874368]{0:T(1024)(128)(4,1)}), s8[4194304]{0:T(1024)(128)(4,1)S(1)}, s32[]{:S(2)}) async-start(s8[18874368]{0:T(1024)(128)(4,1)} %bitcast.7), calls=%async_computation.10 | async-start | bytes 8388608
  17.3 12.5 %slice-start.8 = ((s8[18874368]{0:T(1024)(128)(4,1)}), s8[4194304]{0:T(1024)(128)(4,1)S(1)}, s32[]{:S(2)}) async-start(s8[18874368]{0:T(1024)(128)(4,1)} %bitcast.7), calls=%async_computation.11 | async-start | bytes 8388608
  17.9 1.2 %collective-permute-start = (f32[16,512]{1,0:T(8,128)S(1)}, f32[16,512]{1,0:T(8,128)S(1)}, u32[]{:S(2)}, u32[]{:S(2)}) collective-permute-start(f32[16,512]{1,0:T(8,128)S(1)} %get-tuple-element.10.mine), channel_id=1, source_target_pairs={{0,1},{1,0},{2,3},{3,2},{4,5},{5,4},{6,7},{7,6},{8,9},{9,8},{10,11... | collective-permute-start | bytes 98312 | tf_op jit(solution)/shard_map/ppermute | solution.py:529
  19.1 10.6 %slice-start.4 = ((s8[18874368]{0:T(1024)(128)(4,1)}), s8[2097152]{0:T(1024)(128)(4,1)S(1)}, s32[]{:S(2)}) async-start(s8[18874368]{0:T(1024)(128)(4,1)} %bitcast.5), calls=%async_computation.7 | async-start | bytes 4194304
  19.1 10.6 %slice-start.9 = ((s8[18874368]{0:T(1024)(128)(4,1)}), s8[2097152]{0:T(1024)(128)(4,1)S(1)}, s32[]{:S(2)}) async-start(s8[18874368]{0:T(1024)(128)(4,1)} %bitcast.7), calls=%async_computation.12 | async-start | bytes 4194304
  19.1 10.6 %copy-start = (f32[4096]{0:T(1024)S(1)}, f32[4096]{0:T(1024)}, u32[]{:S(2)}) copy-start(f32[4096]{0:T(1024)} %param.36) | copy-start | bytes 49156
  52.0 1.3 %collective-permute-start.1 = (f32[2,4096]{1,0:T(2,128)S(1)}, f32[2,4096]{1,0:T(2,128)S(1)}, u32[]{:S(2)}, u32[]{:S(2)}) collective-permute-start(f32[2,4096]{1,0:T(2,128)S(1)} %sum.1.mine), channel_id=1, source_target_pairs={{0,1},{1,0},{2,3},{3,2},{4,5},{5,4},{6,7},{7,6},{8,9},{9,8},{10,11... | collective-permute-start | bytes 98312 | tf_op jit(solution)/shard_map/ppermute | solution.py:552

commit v4 on v3

--- a/solution.py
+++ b/solution.py
@@ -148,8 +148,9 @@
 
 
 LANES = 128
-BLOCK = 256
-SLOTS = 5
+BLOCK = 384
+PLAIN = 128
+SLOTS = 2
 EPS = 1e-05
 VMEM = pl.BlockSpec(memory_space=pltpu.VMEM)
 SMEM = pl.BlockSpec(memory_space=pltpu.SMEM)
@@ -287,8 +288,6 @@
 ):
     units, width = gate_weight.shape
     peers, rows, cols = hidden.shape
-    blocks = units // BLOCK
-
     steps = units // BLOCK
     slots = down_buf.shape[0]
 
@@ -302,14 +301,13 @@
         return carry
 
     lax.fori_loop(0, slots, start_copy, 0)
-    half = BLOCK // 2
+    rest = BLOCK - PLAIN
 
     def turn(step):
-        part = pl.ds(step * BLOCK + half, half)
-        turned[step % 2, :, 0:half] = gate_weight[part, :].T
-        turned[step % 2, :, half:] = up_weight[part, :].T
-
-    turn(0)
+        part = pl.ds(step * BLOCK + PLAIN, rest)
+        turned[step % 2, :, 0:rest] = gate_weight[part, :].T
+        turned[step % 2, :, rest:] = up_weight[part, :].T
+
     for d in range(peers):
         wide[:, d * cols : (d + 1) * cols] = hidden[d].astype(F32)
     mean = jnp.sum(wide[...] * wide[...], axis=1, keepdims=True) * (1.0 / width)
@@ -341,12 +339,14 @@
         start = step * BLOCK
         if step + 1 < steps:
             turn(step + 1)
-        part = pl.ds(start, half)
+        part = pl.ds(start, BLOCK if step == 0 else PLAIN)
         gate = lax.dot_general(normed[...], gate_weight[part, :], dims, preferred_element_type=F32)
         up = lax.dot_general(normed[...], up_weight[part, :], dims, preferred_element_type=F32)
         finish(start, gate, up)
+        if step == 0:
+            return
         both = jnp.dot(normed[...], turned[step % 2], preferred_element_type=F32)
-        finish(start + half, both[:, 0:half], both[:, half:])
+        finish(start + PLAIN, both[:, 0:rest], both[:, rest:])
 
     def down_step(step):
         product = jnp.dot(
@@ -399,14 +399,14 @@
         in_specs=[VMEM] * 5 + [ANY],
         out_specs=(VMEM, VMEM),
         scratch_shapes=[
-            pltpu.VMEM((2, width, BLOCK), BF16),
+            pltpu.VMEM((2, width, 2 * (BLOCK - PLAIN)), BF16),
             pltpu.VMEM((SLOTS, BLOCK, width), BF16),
             pltpu.VMEM((all_rows, width), F32),
             pltpu.VMEM((all_rows, width), BF16),
             pltpu.VMEM((all_rows, units), BF16),
             pltpu.SemaphoreType.DMA((SLOTS,)),
         ],
-        compiler_params=pltpu.CompilerParams(vmem_limit_bytes=16 * 2**20),
+        compiler_params=pltpu.CompilerParams(vmem_limit_bytes=17 * 2**20),
         name="experts",
     )(
         hidden,

time: 54.2 us -> 53.4 us (0.985)
  Pallas kernels: 15.7 us -> 14.9 us
    pallas_call x1, Pallas kernels: 12.4 us -> 11.5 us  [run_experts(): pl.pallas_call(expert_kernel, out_shape=(shape((peers, rows, width), BF16...]
where the time goes in v4:
time: 53.4 us; the launch traced here: 53.1 us
  blocking collectives  34.9 us (65%)
  Pallas kernels  14.9 us (28%)
  waiting for transfers between devices  1.71 us (3%)
  between operations  0.81 us (2%)
  local copies, waits for them, and re-layouts  0.76 us (1%)
    all_to_all x1, blocking collectives, fused(): lax.all_to_all(packet, 'expert', split_axis=0, concat_axis=0, tiled=True)  14.5 us
    pallas_call x1, Pallas kernels, run_experts(): pl.pallas_call(expert_kernel, out_shape=(shape((peers, rows, width), BF16...  11.5 us
    all_to_all x1, blocking collectives, fused(): lax.all_to_all(hidden_copies, 'expert', split_axis=0, concat_axis=0, tile...  10.5 us
    all_to_all x1, blocking collectives, fused(): lax.all_to_all(partial_out, 'expert', split_axis=0, concat_axis=0, tiled=...  9.84 us
    pallas_call x1, Pallas kernels, run_mixer(): pl.pallas_call(mixer_kernel, out_shape=(pltpu.VMEM((rows,) + state_pool.s...  2 us
    ppermute x1, waiting for transfers between devices, fused(): other_mixed = lax.ppermute(partial_mixed, 'tensor', swap)  1.22 us
  transfers between devices with their start and end apart: 2, of which 2 were waited for; matrix products, arithmetic and copies ran while one was open for 1% of the time, Pallas kernels for 0%

profile of v4, /device:TPU:0, one launch (start us, length us, event | category | flops | bytes accessed | tf_op | source)
XLA Modules:
  0.0 53.1 jit_solution(17682393251510682283)
XLA Ops:
  0.6 0.0 copy-start.1
  0.6 2.0 %mixer.1 = (bf16[2,16,4096]{2,1,0:T(8,128)(2,1)S(1)}, bf16[8,2,4736]{2,1,0:T(2,128)(2,1)S(1)}) custom-call(s32[2]{0:T(128)} %refs_0_.1, s32[2,2]{1,0:T(2,128)} %refs_1_.1, bf16[2,4096]{1,0:T(2,128)(2,1)} %refs_2_.1, bf16[2,4096]{1,0:T(2,128)(2,1)} %refs_3_.1, bf16[2,4096]{1,0:T(2,128)(2,1)} %refs_4_.1, f32[2,16]{1,0:T(2,128)} %refs_5_.1, f32[2,16]{1,0:T(2,128)} %refs_6_.1, ...), custom_call_target="tpu_custom_call" | custom-call | flops 89999998976 | bytes 300000000 | tf_op jit(solution)/shard_map/mixer/pallas_call | solution.py:443
  2.7 14.5 %all_to_all.15.packets = bf16[8,2,4736]{2,1,0:T(2,128)(2,1)S(1)} all-to-all(bf16[8,2,4736]{2,1,0:T(2,128)(2,1)S(1)} %get-tuple-element.9), channel_id=1, replica_groups=mesh['groups'=2,'expert'=8,'tensor'=2] {'expert'}, dimensions={0} | all-to-all | bytes 303104 | tf_op jit(solution)/shard_map/all_to_all | solution.py:513
  17.2 0.0 copy-done.1
  17.2 0.0 slice-start
  17.2 0.0 slice-start.1
  17.2 0.0 slice-start.3
  17.2 0.0 slice-start.5
  17.2 0.0 slice-start.6
  17.2 0.0 slice-start.7
  17.3 0.0 slice-start.8
  17.3 0.7 %project.1 = (f32[16,512]{1,0:T(8,128)S(1)}, f32[16,512]{1,0:T(8,128)S(1)}, f32[16,128]{1,0:T(8,128)S(1)}) custom-call(bf16[8,2,4736]{2,1,0:T(2,128)(2,1)S(1)} %all_to_all.15.packets, bf16[4096,512]{1,0:T(8,128)(2,1)S(1)} %copy-done.1), custom_call_target="tpu_custom_call" | custom-call | flops 89999998976 | bytes 300000000 | tf_op jit(solution)/shard_map/project/pallas_call | solution.py:514
  17.9 0.0 collective-permute-start
  17.9 1.2 %collective-permute-done.other = f32[16,512]{1,0:T(8,128)S(1)} collective-permute-done((f32[16,512]{1,0:T(8,128)S(1)}, f32[16,512]{1,0:T(8,128)S(1)}, u32[]{:S(2)}, u32[]{:S(2)}) %collective-permute-start) | collective-permute-done | bytes 32800 | tf_op jit(solution)/shard_map/ppermute | solution.py:529
  19.2 10.5 %all_to_all.16.hidden = bf16[8,16,512]{2,1,0:T(8,128)(2,1)S(1)} all-to-all(bf16[8,16,512]{2,1,0:T(8,128)(2,1)S(1)} %hidden.1), channel_id=1, replica_groups=mesh['groups'=2,'expert'=8,'tensor'=2] {'expert'}, dimensions={0} | all-to-all | bytes 262144 | tf_op jit(solution)/shard_map/all_to_all | solution.py:539
  29.7 0.0 slice-done
  29.7 0.0 slice-done.1
  29.7 0.0 slice-done.2
  29.7 0.0 slice-done.3
  29.7 0.0 slice-done.5
  29.7 0.0 slice-done.6
  29.7 0.0 slice-done.7
  29.7 0.0 slice-done.8
  29.7 0.0 slice-done.4
  29.7 0.0 slice-done.9
  29.8 0.0 copy-done
  29.8 11.5 %experts.1 = (bf16[8,2,4096]{2,1,0:T(2,128)(2,1)S(1)}, f32[2,4096]{1,0:T(2,128)S(1)}) custom-call(bf16[8,16,512]{2,1,0:T(8,128)(2,1)S(1)} %all_to_all.16.hidden, f32[16,128]{1,0:T(8,128)S(1)} %get-tuple-element.12.coefs, f32[1,4096]{1,0:T(1,128)S(1)} %bitcast.9, bf16[2304,4096]{1,0:T(8,128)(2,1)S(1)} %bitcast.6, bf16[2304,4096]{1,0:T(8,128)(2,1)S(1)} %bitcast.8, ...), custom_call_target="tpu_custom_call" | custom-call | tf_op jit(solution)/shard_map/experts/pallas_call | solution.py:393
  41.3 9.8 %all_to_all.17.pieces = bf16[8,2,4096]{2,1,0:T(2,128)(2,1)S(1)} all-to-all(bf16[8,2,4096]{2,1,0:T(2,128)(2,1)S(1)} %get-tuple-element.13), channel_id=1, replica_groups=mesh['groups'=2,'expert'=8,'tensor'=2] {'expert'}, dimensions={0} | all-to-all | bytes 262144 | tf_op jit(solution)/shard_map/all_to_all | solution.py:543
  51.2 0.1 collective-permute-start.1
  51.3 0.7 %copy.23 = bf16[2,16,4096]{2,1,0:T(8,128)(2,1)} copy(bf16[2,16,4096]{2,1,0:T(8,128)(2,1)S(1)} %get-tuple-element.17) | data formatting | bytes 524288
  52.0 0.5 collective-permute-done.1.other
  52.5 0.6 %output.1 = bf16[2,4096]{1,0:T(2,128)(2,1)} custom-call(f32[2,4096]{1,0:T(2,128)S(1)} %sum.1.mine, f32[2,4096]{1,0:T(2,128)S(1)} %collective-permute-done.1.other, f32[2,4096]{1,0:T(2,128)S(1)} %get-tuple-element.14.own_rows), custom_call_target="tpu_custom_call" | custom-call | tf_op jit(solution)/shard_map/output/pallas_call | solution.py:553
  (8 shorter events, 0.0 us)
Async XLA Ops:
  0.6 16.6 %copy-start.1 = (bf16[4096,512]{1,0:T(8,128)(2,1)S(1)}, bf16[4096,512]{1,0:T(8,128)(2,1)}, u32[]{:S(2)}) copy-start(bf16[4096,512]{1,0:T(8,128)(2,1)} %out_weight.1) | copy-start | bytes 12582916
  17.2 12.5 %slice-start = ((s8[18874368]{0:T(1024)(128)(4,1)}), s8[4194304]{0:T(1024)(128)(4,1)S(1)}, s32[]{:S(2)}) async-start(s8[18874368]{0:T(1024)(128)(4,1)} %bitcast.5), calls=%async_computation.3 | async-start | bytes 8388608
  17.2 12.5 %slice-start.1 = ((s8[18874368]{0:T(1024)(128)(4,1)}), s8[4194304]{0:T(1024)(128)(4,1)S(1)}, s32[]{:S(2)}) async-start(s8[18874368]{0:T(1024)(128)(4,1)} %bitcast.5), calls=%async_computation.4 | async-start | bytes 8388608
  17.2 12.5 %slice-start.2 = ((s8[18874368]{0:T(1024)(128)(4,1)}), s8[4194304]{0:T(1024)(128)(4,1)S(1)}, s32[]{:S(2)}) async-start(s8[18874368]{0:T(1024)(128)(4,1)} %bitcast.5), calls=%async_computation.5 | async-start | bytes 8388608
  17.2 12.5 %slice-start.3 = ((s8[18874368]{0:T(1024)(128)(4,1)}), s8[4194304]{0:T(1024)(128)(4,1)S(1)}, s32[]{:S(2)}) async-start(s8[18874368]{0:T(1024)(128)(4,1)} %bitcast.5), calls=%async_computation.6 | async-start | bytes 8388608
  17.2 12.5 %slice-start.5 = ((s8[18874368]{0:T(1024)(128)(4,1)}), s8[4194304]{0:T(1024)(128)(4,1)S(1)}, s32[]{:S(2)}) async-start(s8[18874368]{0:T(1024)(128)(4,1)} %bitcast.7), calls=%async_computation.8 | async-start | bytes 8388608
  17.2 12.5 %slice-start.6 = ((s8[18874368]{0:T(1024)(128)(4,1)}), s8[4194304]{0:T(1024)(128)(4,1)S(1)}, s32[]{:S(2)}) async-start(s8[18874368]{0:T(1024)(128)(4,1)} %bitcast.7), calls=%async_computation.9 | async-start | bytes 8388608
  17.2 12.5 %slice-start.7 = ((s8[18874368]{0:T(1024)(128)(4,1)}), s8[4194304]{0:T(1024)(128)(4,1)S(1)}, s32[]{:S(2)}) async-start(s8[18874368]{0:T(1024)(128)(4,1)} %bitcast.7), calls=%async_computation.10 | async-start | bytes 8388608
  17.3 12.5 %slice-start.8 = ((s8[18874368]{0:T(1024)(128)(4,1)}), s8[4194304]{0:T(1024)(128)(4,1)S(1)}, s32[]{:S(2)}) async-start(s8[18874368]{0:T(1024)(128)(4,1)} %bitcast.7), calls=%async_computation.11 | async-start | bytes 8388608
  17.9 1.2 %collective-permute-start = (f32[16,512]{1,0:T(8,128)S(1)}, f32[16,512]{1,0:T(8,128)S(1)}, u32[]{:S(2)}, u32[]{:S(2)}) collective-permute-start(f32[16,512]{1,0:T(8,128)S(1)} %get-tuple-element.10.mine), channel_id=1, source_target_pairs={{0,1},{1,0},{2,3},{3,2},{4,5},{5,4},{6,7},{7,6},{8,9},{9,8},{10,11... | collective-permute-start | bytes 98312 | tf_op jit(solution)/shard_map/ppermute | solution.py:529
  19.1 10.6 %slice-start.4 = ((s8[18874368]{0:T(1024)(128)(4,1)}), s8[2097152]{0:T(1024)(128)(4,1)S(1)}, s32[]{:S(2)}) async-start(s8[18874368]{0:T(1024)(128)(4,1)} %bitcast.5), calls=%async_computation.7 | async-start | bytes 4194304
  19.1 10.6 %slice-start.9 = ((s8[18874368]{0:T(1024)(128)(4,1)}), s8[2097152]{0:T(1024)(128)(4,1)S(1)}, s32[]{:S(2)}) async-start(s8[18874368]{0:T(1024)(128)(4,1)} %bitcast.7), calls=%async_computation.12 | async-start | bytes 4194304
  19.1 10.6 %copy-start = (f32[4096]{0:T(1024)S(1)}, f32[4096]{0:T(1024)}, u32[]{:S(2)}) copy-start(f32[4096]{0:T(1024)} %param.36) | copy-start | bytes 49156
  51.2 1.3 %collective-permute-start.1 = (f32[2,4096]{1,0:T(2,128)S(1)}, f32[2,4096]{1,0:T(2,128)S(1)}, u32[]{:S(2)}, u32[]{:S(2)}) collective-permute-start(f32[2,4096]{1,0:T(2,128)S(1)} %sum.1.mine), channel_id=1, source_target_pairs={{0,1},{1,0},{2,3},{3,2},{4,5},{5,4},{6,7},{7,6},{8,9},{9,8},{10,11... | collective-permute-start | bytes 98312 | tf_op jit(solution)/shard_map/ppermute | solution.py:552
